TPU v7x, 32 devices: a whole 2x2x4 slice. The times are simulated.
32 devices in a mesh: groups: 2 (over y), lon: 4 (over z), lat: 4 (over x, core).
Axes of the slice: x: 2, y: 2, z: 4, core: 2. Of those that a mesh axis runs over, the one named last changes fastest.
Arguments:
- fields: bfloat16 [768, 112, 256], P(('groups', 'lat'), 'lon'), parts along dimension 0, may hold values from -6 to 6
- norm_gains: float32 [3, 256], replicated, may hold values from 0.25 to 1.75
- lon_qkv: bfloat16 [256, 768], replicated, may hold values from -0.375 to 0.375
- lon_out: bfloat16 [256, 256], replicated, may hold values from -0.375 to 0.375
- lat_qkv: bfloat16 [256, 768], replicated, may hold values from -0.375 to 0.375
- lat_out: bfloat16 [256, 256], replicated, may hold values from -0.375 to 0.375
- logit_scales: float32 [2, 8], replicated, may hold values from 0.08 to 7.6
- conv_taps: float32 [25, 256], replicated, may hold values from -1.25 to 1.25
- mlp_in: bfloat16 [256, 2048], replicated, may hold values from -0.375 to 0.375
- mlp_down: bfloat16 [1024, 256], replicated, may hold values from -0.1875 to 0.1875
Outputs:
- mixed_grid: bfloat16 [768, 112, 256], P(('groups', 'lat'), 'lon'), parts along dimension 0
There are 2 independent parts, one for each index of `groups`. A program takes and returns all parts, laid end to end along the dimension named above; an argument that names none is the same for every part. Nothing has to cross between parts.
All inputs are finite; a program needn't handle non-finite values.
Results may differ from a plain program's by a relative error of at most 0.019.
The roundings to bfloat16 on the way count: a program that leaves them out, or rounds other values in their place, can miss the bound.
Values may be sent and summed in bfloat16 or wider, within the bound.
A program may use at most 64 MiB of HBM per device.

v0:
```python
import jax
import jax.numpy as jnp
from jax import lax
from jax.sharding import PartitionSpec as P

KERNEL = 5


EPSILON = 1e-05
EINSUM_FORMS = {
    "second": ("rlf,rmf->rlm", "iwr,irq->iwq"),
    "first": ("ugv,ngv->gun", "opu,uoj->opj"),
}


def extended(x, sides, width, wrap):
    for axis, dim in sides:
        count, length = (lax.axis_size(axis), x.shape[dim])
        up = [(i, (i + 1) % count) for i in range(count if wrap else count - 1)]
        down = [(j, i) for i, j in up]
        last = lax.slice_in_dim(x, length - width, length, axis=dim)
        leading = lax.slice_in_dim(x, 0, width, axis=dim)
        before = lax.ppermute(last, axis, up)
        after = lax.ppermute(leading, axis, down)
        x = jnp.concatenate([before, x, after], axis=dim)
    return x


def layer_norm(values, gains):
    average = jnp.mean(values, -1, keepdims=True)
    centred = values - average
    spread = jnp.mean(centred * centred, -1, keepdims=True)
    return centred * lax.rsqrt(spread + EPSILON) * gains


def project(inputs, weight):
    leading = inputs.shape[:-1]
    flat = inputs.reshape(-1, inputs.shape[-1])
    return jnp.dot(flat, weight, preferred_element_type=jnp.float32).reshape(
        leading + (weight.shape[1],)
    )


def split_heads(packed, heads):
    shaped = packed.reshape(packed.shape[:-1] + (heads, packed.shape[-1] // heads))
    return jnp.moveaxis(shaped, -2, 0)


def initial_state(queries, form):
    heads, first_len, second_len, head_size = queries.shape
    if form == "second":
        batch_len, length = (first_len, second_len)
    else:
        batch_len, length = (second_len, first_len)
    return (
        jnp.full((heads, batch_len, length), -1e30, jnp.float32),
        jnp.zeros((heads, batch_len, length), jnp.float32),
        jnp.zeros((heads, batch_len, length, head_size), jnp.float32),
    )


def head_step(state, queries, keys_in, values_in, factor, form):
    running_max, running_sum, running_acc = state
    scores = (
        jnp.einsum(EINSUM_FORMS[form][0], queries, keys_in, preferred_element_type=jnp.float32)
        * factor
    )
    new_max = jnp.maximum(running_max, jnp.max(scores, -1))
    fading = jnp.exp(running_max - new_max)
    weights = jnp.exp(scores - new_max[..., None])
    running_sum = running_sum * fading + jnp.sum(weights, -1)
    running_acc = running_acc * fading[..., None] + jnp.einsum(
        EINSUM_FORMS[form][1],
        weights.astype(jnp.bfloat16),
        values_in,
        preferred_element_type=jnp.float32,
    )
    return (new_max, running_sum, running_acc)


def attend_heads(state, queries, keys_in, values_in, factors, form):

    def one_head(packed):
        return head_step(packed[0], packed[1], packed[2], packed[3], packed[4], form)

    return lax.map(one_head, (state, queries, keys_in, values_in, factors))


def finish(state, form, out_weight):
    running_max, running_sum, running_acc = state
    mixed_out = running_acc / running_sum[..., None]
    order = (1, 2, 0, 3) if form == "second" else (2, 1, 0, 3)
    mixed_out = jnp.transpose(mixed_out, order)
    mixed_out = mixed_out.reshape(mixed_out.shape[:2] + (-1,)).astype(jnp.bfloat16)
    return project(mixed_out, out_weight).astype(jnp.bfloat16)


def full_attention(normed, qkv_weight, out_weight, factors, form):
    features = normed.shape[-1]
    heads = factors.shape[0]
    qkv_all = project(normed, qkv_weight).astype(jnp.bfloat16)
    queries = split_heads(qkv_all[..., :features], heads)
    keys_in = split_heads(qkv_all[..., features : 2 * features], heads)
    values_in = split_heads(qkv_all[..., 2 * features :], heads)
    state = attend_heads(initial_state(queries, form), queries, keys_in, values_in, factors, form)
    return finish(state, form, out_weight)


def per_device(
    fields,
    norm_gains,
    lon_qkv,
    lon_out,
    lat_qkv,
    lat_out,
    logit_scales,
    conv_taps,
    mlp_in,
    mlp_down,
):
    lat_rows, lon_cols, features = fields.shape
    anchor = fields.astype(jnp.float32)
    normed = layer_norm(anchor, norm_gains[0]).astype(jnp.bfloat16)
    lon_count = lax.axis_size("lon")
    stacked = normed.reshape(lon_count, lat_rows // lon_count, lon_cols, features)
    exchanged = lax.all_to_all(stacked, "lon", split_axis=0, concat_axis=2, tiled=True)
    line_set = exchanged.reshape(exchanged.shape[1], exchanged.shape[2], features)
    mixed_out = full_attention(line_set, lon_qkv, lon_out, logit_scales[0], "second")
    lon_mix = lax.all_to_all(
        mixed_out.reshape(exchanged.shape), "lon", split_axis=2, concat_axis=0, tiled=True
    ).reshape(lat_rows, lon_cols, features)
    first_state = (anchor + lon_mix.astype(jnp.float32)).astype(jnp.bfloat16)
    first_wide = first_state.astype(jnp.float32)
    normed = layer_norm(first_wide, norm_gains[1]).astype(jnp.bfloat16)
    band_count = lax.axis_size("lat")
    stacked = normed.reshape(lat_rows, band_count, lon_cols // band_count, features)
    exchanged = lax.all_to_all(stacked, "lat", split_axis=1, concat_axis=0, tiled=True)
    line_set = exchanged.reshape(exchanged.shape[0], exchanged.shape[2], features)
    mixed_out = full_attention(line_set, lat_qkv, lat_out, logit_scales[1], "first")
    lat_mix = lax.all_to_all(
        mixed_out.reshape(exchanged.shape), "lat", split_axis=0, concat_axis=1, tiled=True
    ).reshape(lat_rows, lon_cols, features)
    second_state = (first_wide + lat_mix.astype(jnp.float32)).astype(jnp.bfloat16)
    margin = KERNEL // 2
    widened = extended(second_state, (("lon", 1),), margin, True)
    widened = extended(widened, (("lat", 0),), margin, False).astype(jnp.float32)
    smoothed = jnp.zeros((lat_rows, lon_cols, features), jnp.float32)
    for row_tap in range(KERNEL):
        for col_tap in range(KERNEL):
            smoothed = (
                smoothed
                + conv_taps[row_tap * KERNEL + col_tap]
                * widened[row_tap : row_tap + lat_rows, col_tap : col_tap + lon_cols]
            )
    normed = layer_norm(smoothed, norm_gains[2]).astype(jnp.bfloat16)
    hidden_len = mlp_down.shape[0]
    gate_up = jnp.dot(normed.reshape(-1, features), mlp_in, preferred_element_type=jnp.float32)
    hidden = (jax.nn.silu(gate_up[:, :hidden_len]) * gate_up[:, hidden_len:]).astype(jnp.bfloat16)
    update = jnp.dot(hidden, mlp_down, preferred_element_type=jnp.float32).reshape(
        lat_rows, lon_cols, features
    )
    return (second_state.astype(jnp.float32) + update).astype(jnp.bfloat16)


def solution(mesh):
    in_specs = (P(("groups", "lat"), "lon", None), P(), P(), P(), P(), P(), P(), P(), P(), P())
    out_specs = P(("groups", "lat"), "lon", None)
    return jax.shard_map(
        per_device, mesh=mesh, in_specs=in_specs, out_specs=out_specs, check_vma=False
    )
```

profile of v0, /device:TPU:25, one launch (start us, length us, event | category | flops | bytes accessed | tf_op | source)
XLA Modules:
  0.0 309.7 jit_solution(7108615203687747032)
XLA Ops:
  7.2 4.5 %all-to-all-start = ((bf16[4,24,28,256]{3,1,2,0:T(8,128)(2,1)}), bf16[4,24,28,256]{3,1,2,0:T(8,128)(2,1)}, u32[]{:S(2)}, u32[]{:S(2)}) async-start(bf16[4,24,28,256]{3,1,2,0:T(8,128)(2,1)} %copy.106), calls=%async_computation | async-start | bytes 2752512 | tf_op jit(solution)/shard_map/all_to_all | solution.py:126
  11.8 29.9 %all-to-all-done = bf16[4,24,28,256]{3,1,2,0:T(8,128)(2,1)} async-done(((bf16[4,24,28,256]{3,1,2,0:T(8,128)(2,1)}), bf16[4,24,28,256]{3,1,2,0:T(8,128)(2,1)}, u32[]{:S(2)}, u32[]{:S(2)}) %all-to-all-start) | async-done | bytes 1376288 | tf_op jit(solution)/shard_map/all_to_all | solution.py:126
  54.0 39.9 %while.24 = (s32[]{:T(128)}, f32[8,24,112]{2,1,0:T(8,128)S(1)}, f32[8,24,112,32]{2,3,1,0:T(8,128)}, bf16[8,24,112,32]{2,3,0,1:T(8,128)(2,1)}, bf16[8,24,112,32]{...) while((s32[]{:T(128)}, f32[8,24,112]{2,1,0:T(8,128)S(1)}, ...), condition=%wide.region_5.6_spmd, body=%wide.region_2.5_spmd.sunk | while | flops 40440960 | bytes 4721261 | solution.py:86
  98.3 35.1 %all_to_all.48 = bf16[1,24,112,256]{3,1,0,2:T(8,128)(2,1)S(1)} all-to-all(bf16[1,24,112,256]{3,1,0,2:T(8,128)(2,1)S(1)} %copy.116), channel_id=1, replica_groups=mesh['groups'=2,'lon'=4,'lat'=4] {'lon'}, dimensions={2} | all-to-all | bytes 2752512 | tf_op jit(solution)/shard_map/all_to_all | solution.py:129
  137.3 5.1 %all-to-all-start.2 = ((bf16[96,4,7,256]{3,0,2,1:T(8,128)(2,1)}), bf16[96,4,7,256]{3,0,2,1:T(8,128)(2,1)S(1)}, u32[]{:S(2)}, u32[]{:S(2)}) async-start(bf16[96,4,7,256]{3,0,2,1:T(8,128)(2,1)} %bitcast.182), calls=%async_computation.2 | async-start | bytes 2752512 | tf_op jit(solution)/shard_map/all_to_all | solution.py:137
  142.4 17.1 %all-to-all-done.2 = bf16[96,4,7,256]{3,0,2,1:T(8,128)(2,1)S(1)} async-done(((bf16[96,4,7,256]{3,0,2,1:T(8,128)(2,1)}), bf16[96,4,7,256]{3,0,2,1:T(8,128)(2,1)S(1)}, u32[]{:S(2)}, u32[]{:S(2)}) %all-to-all-start.2) | async-done | bytes 1376288 | tf_op jit(solution)/shard_map/all_to_all | solution.py:137
  169.6 61.0 %while.25 = (s32[]{:T(128)}, f32[8,7,384]{2,0,1:T(8,128)S(1)}, f32[8,7,384,32]{2,3,0,1:T(8,128)}, bf16[8,384,7,32]{1,3,0,2:T(8,128)(2,1)}, bf16[8,384,7,32]{1,3,...) while((s32[]{:T(128)}, f32[8,7,384]{2,0,1:T(8,128)S(1)}, ...), condition=%wide.region_11.12_spmd, body=%wide.region_8.11_spmd.sunk | while | flops 140472192 | bytes 13410937 | solution.py:86
  174.0 3.1 %fusion.119 = f32[8,7,384,32]{2,3,0,1:T(8,128)} fusion(f32[8,7,384,32]{2,3,0,1:T(8,128)} %get-tuple-element.358, s32[]{:T(128)S(6)} %copy.177, f32[7,384,384]{1,2,0:T(8,128)S(1)} %get-tuple-element.320, f32[7,384]{1,0:T(8,128)S(1)} %broadcast_maximum_fusion.3, f32[]{:T(128)} %bitcast.177, bf16[8,384,7,32]{1,3,0,2:T(8,128)(2,1)} %get-tuple-element.371, ...), kind=kOutput, calls=%fused_computation.26.clone.1 | convolution fusion | flops 69242880 | bytes 4667904 | tf_op jit(solution)/shard_map/while/body/eval_jaxpr/opu,uoj->opj/dot_general | solution.py:72
  181.6 3.1 %fusion.119 = f32[8,7,384,32]{2,3,0,1:T(8,128)} fusion(f32[8,7,384,32]{2,3,0,1:T(8,128)} %get-tuple-element.358, s32[]{:T(128)S(6)} %copy.177, f32[7,384,384]{1,2,0:T(8,128)S(1)} %get-tuple-element.320, f32[7,384]{1,0:T(8,128)S(1)} %broadcast_maximum_fusion.3, f32[]{:T(128)} %bitcast.177, bf16[8,384,7,32]{1,3,0,2:T(8,128)(2,1)} %get-tuple-element.371, ...), kind=kOutput, calls=%fused_computation.26.clone.1 | convolution fusion | flops 69242880 | bytes 4667904 | tf_op jit(solution)/shard_map/while/body/eval_jaxpr/opu,uoj->opj/dot_general | solution.py:72
  189.3 3.2 %fusion.119 = f32[8,7,384,32]{2,3,0,1:T(8,128)} fusion(f32[8,7,384,32]{2,3,0,1:T(8,128)} %get-tuple-element.358, s32[]{:T(128)S(6)} %copy.177, f32[7,384,384]{1,2,0:T(8,128)S(1)} %get-tuple-element.320, f32[7,384]{1,0:T(8,128)S(1)} %broadcast_maximum_fusion.3, f32[]{:T(128)} %bitcast.177, bf16[8,384,7,32]{1,3,0,2:T(8,128)(2,1)} %get-tuple-element.371, ...), kind=kOutput, calls=%fused_computation.26.clone.1 | convolution fusion | flops 69242880 | bytes 4667904 | tf_op jit(solution)/shard_map/while/body/eval_jaxpr/opu,uoj->opj/dot_general | solution.py:72
  196.9 3.1 %fusion.119 = f32[8,7,384,32]{2,3,0,1:T(8,128)} fusion(f32[8,7,384,32]{2,3,0,1:T(8,128)} %get-tuple-element.358, s32[]{:T(128)S(6)} %copy.177, f32[7,384,384]{1,2,0:T(8,128)S(1)} %get-tuple-element.320, f32[7,384]{1,0:T(8,128)S(1)} %broadcast_maximum_fusion.3, f32[]{:T(128)} %bitcast.177, bf16[8,384,7,32]{1,3,0,2:T(8,128)(2,1)} %get-tuple-element.371, ...), kind=kOutput, calls=%fused_computation.26.clone.1 | convolution fusion | flops 69242880 | bytes 4667904 | tf_op jit(solution)/shard_map/while/body/eval_jaxpr/opu,uoj->opj/dot_general | solution.py:72
  204.5 3.1 %fusion.119 = f32[8,7,384,32]{2,3,0,1:T(8,128)} fusion(f32[8,7,384,32]{2,3,0,1:T(8,128)} %get-tuple-element.358, s32[]{:T(128)S(6)} %copy.177, f32[7,384,384]{1,2,0:T(8,128)S(1)} %get-tuple-element.320, f32[7,384]{1,0:T(8,128)S(1)} %broadcast_maximum_fusion.3, f32[]{:T(128)} %bitcast.177, bf16[8,384,7,32]{1,3,0,2:T(8,128)(2,1)} %get-tuple-element.371, ...), kind=kOutput, calls=%fused_computation.26.clone.1 | convolution fusion | flops 69242880 | bytes 4667904 | tf_op jit(solution)/shard_map/while/body/eval_jaxpr/opu,uoj->opj/dot_general | solution.py:72
  212.2 3.1 %fusion.119 = f32[8,7,384,32]{2,3,0,1:T(8,128)} fusion(f32[8,7,384,32]{2,3,0,1:T(8,128)} %get-tuple-element.358, s32[]{:T(128)S(6)} %copy.177, f32[7,384,384]{1,2,0:T(8,128)S(1)} %get-tuple-element.320, f32[7,384]{1,0:T(8,128)S(1)} %broadcast_maximum_fusion.3, f32[]{:T(128)} %bitcast.177, bf16[8,384,7,32]{1,3,0,2:T(8,128)(2,1)} %get-tuple-element.371, ...), kind=kOutput, calls=%fused_computation.26.clone.1 | convolution fusion | flops 69242880 | bytes 4667904 | tf_op jit(solution)/shard_map/while/body/eval_jaxpr/opu,uoj->opj/dot_general | solution.py:72
  219.8 3.1 %fusion.119 = f32[8,7,384,32]{2,3,0,1:T(8,128)} fusion(f32[8,7,384,32]{2,3,0,1:T(8,128)} %get-tuple-element.358, s32[]{:T(128)S(6)} %copy.177, f32[7,384,384]{1,2,0:T(8,128)S(1)} %get-tuple-element.320, f32[7,384]{1,0:T(8,128)S(1)} %broadcast_maximum_fusion.3, f32[]{:T(128)} %bitcast.177, bf16[8,384,7,32]{1,3,0,2:T(8,128)(2,1)} %get-tuple-element.371, ...), kind=kOutput, calls=%fused_computation.26.clone.1 | convolution fusion | flops 69242880 | bytes 4667904 | tf_op jit(solution)/shard_map/while/body/eval_jaxpr/opu,uoj->opj/dot_general | solution.py:72
  227.4 3.1 %fusion.119 = f32[8,7,384,32]{2,3,0,1:T(8,128)} fusion(f32[8,7,384,32]{2,3,0,1:T(8,128)} %get-tuple-element.358, s32[]{:T(128)S(6)} %copy.177, f32[7,384,384]{1,2,0:T(8,128)S(1)} %get-tuple-element.320, f32[7,384]{1,0:T(8,128)S(1)} %broadcast_maximum_fusion.3, f32[]{:T(128)} %bitcast.177, bf16[8,384,7,32]{1,3,0,2:T(8,128)(2,1)} %get-tuple-element.371, ...), kind=kOutput, calls=%fused_computation.26.clone.1 | convolution fusion | flops 69242880 | bytes 4667904 | tf_op jit(solution)/shard_map/while/body/eval_jaxpr/opu,uoj->opj/dot_general | solution.py:72
  234.3 22.4 %all_to_all.49 = bf16[384,1,7,256]{3,2,1,0:T(8,128)(2,1)S(1)} all-to-all(bf16[384,1,7,256]{3,2,1,0:T(8,128)(2,1)S(1)} %copy.129), channel_id=1, replica_groups=mesh['groups'=2,'lon'=4,'lat'=4] {'lat'}, dimensions={0} | all-to-all | bytes 2752512 | tf_op jit(solution)/shard_map/all_to_all | solution.py:140
  262.9 3.6 %collective-permute-done.1 = bf16[96,2,256]{2,0,1:T(8,128)(2,1)S(1)} collective-permute-done((bf16[96,2,256]{2,0,1:T(8,128)(2,1)S(1)}, bf16[96,2,256]{2,0,1:T(8,128)(2,1)S(1)}, u32[]{:S(2)}, u32[]{:S(2)}) %collective-permute-start.1) | collective-permute-done | bytes 98336 | tf_op jit(solution)/shard_map/ppermute | solution.py:24
  266.6 4.3 %collective-permute-start.2 = (bf16[2,32,256]{2,0,1:T(2,128)(2,1)S(1)}, bf16[2,32,256]{2,0,1:T(2,128)(2,1)S(1)}, u32[]{:S(2)}, u32[]{:S(2)}) collective-permute-start(bf16[2,32,256]{2,0,1:T(2,128)(2,1)S(1)} %get-tuple-element.187), channel_id=1, source_target_pairs={{0,1},{1,2},{2,3},{4,5},{5,6},{6,7},{8,9},{9,10},{10,11},{12,13},{... | collective-permute-start | bytes 98312 | tf_op jit(solution)/shard_map/ppermute | solution.py:23
  276.8 8.6 %fusion.85 = (f32[96,28]{0,1:T(8,128)S(1)}, f32[96,28,256]{2,0,1:T(8,128)S(1)}) fusion(f32[100,32,256]{2,0,1:T(8,128)S(1)} %maximum_convert_fusion, f32[256]{0:T(256)S(1)} %bitcast.218, f32[256]{0:T(256)S(1)} %bitcast.219, f32[256]{0:T(256)S(1)} %bitcast.196, f32[256]{0:T(256)S(1)} %bitcast.197, f32[256]{0:T(256)S(1)} %bitcast.198, f32[256]{0:T(256)S(1)} %bitcast.199, ...), kind=kLoop, calls=%fused_computation.142 | loop fusion | flops 34403712 | bytes 71601664 | tf_op jit(solution)/shard_map/reduce_sum | solution.py:30
  289.2 3.3 %reshape.220 = bf16[2688,256]{1,0:T(8,128)(2,1)} reshape(bf16[96,28,256]{2,1,0:T(8,128)(2,1)} %copy.132) | data formatting | bytes 2752512 | tf_op jit(solution)/shard_map/reshape | solution.py:157
  292.5 4.4 %fusion.95 = f32[2688,2048]{1,0:T(8,128)S(1)} fusion(bf16[2688,256]{1,0:T(8,128)(2,1)} %reshape.220, bf16[256,2048]{1,0:T(8,128)(2,1)S(1)} %copy-done), kind=kOutput, calls=%fused_computation.150 | convolution fusion | flops 2818572288 | bytes 24444928 | tf_op jit(solution)/shard_map/dot_general | solution.py:157
  296.9 4.3 %fusion.37 = f32[2688,256]{1,0:T(8,128)} fusion(bf16[1024,256]{1,0:T(8,128)(2,1)S(1)} %copy-done.10, f32[2688,2048]{1,0:T(8,128)S(1)} %fusion.95), kind=kOutput, calls=%fused_computation.41 | convolution fusion | flops 1425801216 | bytes 25296896 | tf_op jit(solution)/shard_map/dot_general | solution.py:159
  301.2 4.0 %reshape.221 = f32[96,28,256]{2,1,0:T(8,128)} reshape(f32[2688,256]{1,0:T(8,128)} %fusion.37) | data formatting | bytes 5505024 | tf_op jit(solution)/shard_map/reshape | solution.py:159
  305.2 4.5 %fusion.75 = bf16[96,28,256]{2,0,1:T(8,128)(2,1)} fusion(f32[96,28,256]{2,1,0:T(8,128)} %reshape.221, bf16[96,28,256]{2,0,1:T(8,128)(2,1)S(1)} %fusion.50), kind=kLoop, calls=%fused_computation.113 | loop fusion | flops 2064384 | bytes 5505024 | tf_op jit(solution)/shard_map/convert_element_type | solution.py:162
  (183 shorter events, 132.8 us)
Async XLA Ops:
  0.0 292.5 %copy-start = (bf16[256,2048]{1,0:T(8,128)(2,1)S(1)}, bf16[256,2048]{1,0:T(8,128)(2,1)}, u32[]{:S(2)}) copy-start(bf16[256,2048]{1,0:T(8,128)(2,1)} %param.22) | copy-start | bytes 3145732
  0.0 5.1 %copy-start.1 = (bf16[96,28,256]{2,0,1:T(8,128)(2,1)S(1)}, bf16[96,28,256]{2,0,1:T(8,128)(2,1)}, u32[]{:S(2)}) copy-start(bf16[96,28,256]{2,0,1:T(8,128)(2,1)} %param.14) | copy-start | bytes 4128772
  6.0 5.7 %copy-start.9 = (f32[2,8]{1,0:T(2,128)S(1)}, f32[2,8]{1,0:T(2,128)}, u32[]{:S(2)}) copy-start(f32[2,8]{1,0:T(2,128)} %param.20) | copy-start | bytes 196
  6.0 35.6 %copy-start.4 = (bf16[256,768]{1,0:T(8,128)(2,1)S(1)}, bf16[256,768]{1,0:T(8,128)(2,1)}, u32[]{:S(2)}) copy-start(bf16[256,768]{1,0:T(8,128)(2,1)} %param.16) | copy-start | bytes 1179652
  7.2 34.4 %all-to-all-start = ((bf16[4,24,28,256]{3,1,2,0:T(8,128)(2,1)}), bf16[4,24,28,256]{3,1,2,0:T(8,128)(2,1)}, u32[]{:S(2)}, u32[]{:S(2)}) async-start(bf16[4,24,28,256]{3,1,2,0:T(8,128)(2,1)} %copy.106), calls=%async_computation | async-start | bytes 2752512 | tf_op jit(solution)/shard_map/all_to_all | solution.py:126
  96.2 0.9 copy-start.6
  134.5 1.1 copy-start.2
  137.3 22.3 %copy-start.5 = (bf16[256,768]{1,0:T(8,128)(2,1)S(1)}, bf16[256,768]{1,0:T(8,128)(2,1)}, u32[]{:S(2)}) copy-start(bf16[256,768]{1,0:T(8,128)(2,1)} %param.18) | copy-start | bytes 1179652
  137.3 22.2 %all-to-all-start.2 = ((bf16[96,4,7,256]{3,0,2,1:T(8,128)(2,1)}), bf16[96,4,7,256]{3,0,2,1:T(8,128)(2,1)S(1)}, u32[]{:S(2)}, u32[]{:S(2)}) async-start(bf16[96,4,7,256]{3,0,2,1:T(8,128)(2,1)} %bitcast.182), calls=%async_computation.2 | async-start | bytes 2752512 | tf_op jit(solution)/shard_map/all_to_all | solution.py:137
  230.7 2.2 copy-start.7
  257.2 1.3 copy-start.3
  258.6 2.7 copy-start.8
  259.1 3.9 %collective-permute-start = (bf16[96,2,256]{2,0,1:T(8,128)(2,1)S(1)}, bf16[96,2,256]{2,0,1:T(8,128)(2,1)S(1)}, u32[]{:S(2)}, u32[]{:S(2)}) collective-permute-start(bf16[96,2,256]{2,0,1:T(8,128)(2,1)S(1)} %get-tuple-element.189), channel_id=1, source_target_pairs={{0,4},{4,8},{8,12},{12,0},{1,5},{5,9},{9,13},{13,1},{2,6},{6,10},{... | collective-permute-start | bytes 294920 | tf_op jit(solution)/shard_map/ppermute | solution.py:23
  261.3 5.3 %collective-permute-start.1 = (bf16[96,2,256]{2,0,1:T(8,128)(2,1)S(1)}, bf16[96,2,256]{2,0,1:T(8,128)(2,1)S(1)}, u32[]{:S(2)}, u32[]{:S(2)}) collective-permute-start(bf16[96,2,256]{2,0,1:T(8,128)(2,1)S(1)} %get-tuple-element.190), channel_id=1, source_target_pairs={{4,0},{8,4},{12,8},{0,12},{5,1},{9,5},{13,9},{1,13},{6,2},{10,6},{... | collective-permute-start | bytes 294920 | tf_op jit(solution)/shard_map/ppermute | solution.py:24
  266.6 6.5 %collective-permute-start.2 = (bf16[2,32,256]{2,0,1:T(2,128)(2,1)S(1)}, bf16[2,32,256]{2,0,1:T(2,128)(2,1)S(1)}, u32[]{:S(2)}, u32[]{:S(2)}) collective-permute-start(bf16[2,32,256]{2,0,1:T(2,128)(2,1)S(1)} %get-tuple-element.187), channel_id=1, source_target_pairs={{0,1},{1,2},{2,3},{4,5},{5,6},{6,7},{8,9},{9,10},{10,11},{12,13},{... | collective-permute-start | bytes 98312 | tf_op jit(solution)/shard_map/ppermute | solution.py:23
  271.0 5.2 %collective-permute-start.3 = (bf16[2,32,256]{2,0,1:T(2,128)(2,1)S(1)}, bf16[2,32,256]{2,0,1:T(2,128)(2,1)S(1)}, u32[]{:S(2)}, u32[]{:S(2)}) collective-permute-start(bf16[2,32,256]{2,0,1:T(2,128)(2,1)S(1)} %get-tuple-element.188), channel_id=1, source_target_pairs={{1,0},{2,1},{3,2},{5,4},{6,5},{7,6},{9,8},{10,9},{11,10},{13,12},{... | collective-permute-start | bytes 98312 | tf_op jit(solution)/shard_map/ppermute | solution.py:24
  292.5 4.4 %copy-start.10 = (bf16[1024,256]{1,0:T(8,128)(2,1)S(1)}, bf16[1024,256]{1,0:T(8,128)(2,1)}, u32[]{:S(2)}) copy-start(bf16[1024,256]{1,0:T(8,128)(2,1)} %param.23) | copy-start | bytes 1572868
where the time goes:
time: 313 us; the launch traced here: 310 us
  matrix products  90.6 us (29%)
  blocking collectives  57.4 us (18%)
  waiting for transfers between devices  55.3 us (18%)
  local copies, waits for them, and re-layouts  44.8 us (14%)
  other arithmetic  42.3 us (14%)
  starting transfers between devices  18.3 us (6%)
    dot_general x16, matrix products, head_step(): jnp.einsum(EINSUM_FORMS[form][1], weights.astype(jnp.bfloat16), values_in...  41 us
    dot_general x16, matrix products, head_step(): jnp.einsum(EINSUM_FORMS[form][0], queries, keys_in, preferred_element_typ...  35.9 us
    all_to_all x1, blocking collectives, per_device(): lax.all_to_all(mixed_out.reshape(exchanged.shape), 'lon', split_axis=2, c...  35.1 us
    all_to_all x1, waiting for transfers between devices, per_device(): lax.all_to_all(stacked, 'lon', split_axis=0, concat_axis=2, tiled=True)  29.9 us
    all_to_all x1, blocking collectives, per_device(): lax.all_to_all(mixed_out.reshape(exchanged.shape), 'lat', split_axis=0, c...  22.4 us
    all_to_all x1, waiting for transfers between devices, per_device(): lax.all_to_all(stacked, 'lat', split_axis=1, concat_axis=0, tiled=True)  17.1 us
    reduce_sum x16, other arithmetic, head_step(): running_sum = running_sum * fading + jnp.sum(weights, -1)  12.5 us
    reduce_sum x3, other arithmetic, layer_norm(): average = jnp.mean(values, -1, keepdims=True)  11.1 us
  transfers between devices with their start and end apart: 6, of which 5 were waited for; matrix products, arithmetic and copies ran while one was open for 0% of the time, Pallas kernels for 0%

commit v1 on v0

v1 whole, which is shorter than its diff:
```python
import functools
import math

import jax
import jax.numpy as jnp
from jax import lax
from jax.experimental import pallas as pl
from jax.experimental.pallas import tpu as pltpu
from jax.sharding import PartitionSpec as P

KERNEL = 5
LANES = 128
EPSILON = 1e-05
MESH = pl.DeviceIdType.MESH
F32, BF16 = jnp.float32, jnp.bfloat16
NT = (((1,), (1,)), ((), ()))
TN = (((0,), (0,)), ((), ()))


def extended(x, sides, width, wrap):
    for axis, dim in sides:
        count, length = (lax.axis_size(axis), x.shape[dim])
        up = [(i, (i + 1) % count) for i in range(count if wrap else count - 1)]
        down = [(j, i) for i, j in up]
        last = lax.slice_in_dim(x, length - width, length, axis=dim)
        leading = lax.slice_in_dim(x, 0, width, axis=dim)
        before = lax.ppermute(last, axis, up)
        after = lax.ppermute(leading, axis, down)
        x = jnp.concatenate([before, x, after], axis=dim)
    return x


def layer_norm(values, gains):
    average = jnp.mean(values, -1, keepdims=True)
    centred = values - average
    spread = jnp.mean(centred * centred, -1, keepdims=True)
    return centred * lax.rsqrt(spread + EPSILON) * gains


def attend(x, wqk, wvt, wout, factor_of, heads, valid):
    features = x.shape[-1]
    size = features // heads
    qk = jnp.dot(x, wqk, preferred_element_type=F32).astype(BF16)
    queries, keys = qk[:, :features], qk[:, features:]
    values = lax.dot_general(wvt, x, NT, preferred_element_type=F32).astype(BF16)
    lane = lax.broadcasted_iota(jnp.int32, (1, features), 1) // size
    parts = []
    for h in range(heads):
        own = keys * (lane == h).astype(F32).astype(BF16)
        scores = lax.dot_general(own, queries, NT, preferred_element_type=F32)
        if valid is not None:
            scores = jnp.where(valid, scores, -1e30)
        top = jnp.max(scores, 0, keepdims=True)
        weights = jnp.exp2((scores - top) * (factor_of(h) * math.log2(math.e)))
        total = jnp.sum(weights, 0, keepdims=True)
        part = jnp.dot(
            values[h * size : (h + 1) * size], weights.astype(BF16), preferred_element_type=F32
        )
        parts.append(part / total)
    context = jnp.concatenate(parts, 0).astype(BF16)
    return lax.dot_general(context, wout, TN, preferred_element_type=F32).astype(BF16)


def attention_kernel(
    n, m, heads, lon_cols, chunk,
    x_ref, gains, wqk1, wvt1, wo1, wqk2, wvt2, wo2, scales,
    out_ref,
    xs, recv, obuf, ret, normed, state, lsend, lrecv, lout, lret,
    fs, fr, bs, br, gs, gr, hs, hr,
):
    rows_own = xs.shape[1]
    width, features = xs.shape[2], xs.shape[3]
    chunks = rows_own // chunk
    band = chunk * n
    lat_rows = rows_own * n
    cols_own = lon_cols // m
    halves = features // LANES
    me = lax.axis_index("lon")
    mine = lax.axis_index("lat")
    lon_peers = [lax.rem(me + d, n) for d in range(1, n)]
    lat_peers = [lax.rem(mine + d, m) for d in range(1, m)]

    barrier = pltpu.get_barrier_semaphore()
    for peer in lon_peers:
        pl.semaphore_signal(barrier, inc=1, device_id={"lon": peer}, device_id_type=MESH)
    for peer in lat_peers:
        pl.semaphore_signal(barrier, inc=1, device_id={"lat": peer}, device_id_type=MESH)
    pl.semaphore_wait(barrier, n + m - 2)

    def forth(ch, d):
        peer = lon_peers[d]
        part = pl.ds(ch * chunk, chunk)
        return pltpu.make_async_remote_copy(
            src_ref=xs.at[peer, part], dst_ref=recv.at[me, part],
            send_sem=fs.at[ch, d], recv_sem=fr.at[ch, d],
            device_id={"lon": peer}, device_id_type=MESH,
        )

    def back(ch, d):
        peer = lon_peers[d]
        part = pl.ds(ch * chunk, chunk)
        return pltpu.make_async_remote_copy(
            src_ref=obuf.at[peer, part], dst_ref=ret.at[me, part],
            send_sem=bs.at[ch, d], recv_sem=br.at[ch, d],
            device_id={"lon": peer}, device_id_type=MESH,
        )

    def lat_forth(ch, d):
        peer = lat_peers[d]
        part = pl.ds(pl.multiple_of(ch * band, band), band)
        return pltpu.make_async_remote_copy(
            src_ref=lsend.at[pl.ds(peer * cols_own, cols_own), part],
            dst_ref=lrecv.at[mine, pl.ds(0, cols_own), part],
            send_sem=gs.at[ch, d], recv_sem=gr.at[ch, d],
            device_id={"lat": peer}, device_id_type=MESH,
        )

    def lat_back(c, d):
        peer = lat_peers[d]
        return pltpu.make_async_remote_copy(
            src_ref=lout.at[peer, c], dst_ref=lret.at[mine * cols_own + c],
            send_sem=hs.at[c, d], recv_sem=hr.at[c, d],
            device_id={"lat": peer}, device_id_type=MESH,
        )

    @pl.loop(0, chunks)
    def _(ch):
        part = pl.ds(ch * chunk, chunk)
        for o in range(n):
            block = x_ref[pl.ds(o * rows_own + ch * chunk, chunk)].astype(F32)
            xs[o, part] = layer_norm(block, gains[0:1][None]).astype(BF16)
        for d in range(n - 1):
            forth(ch, d).start()
        recv[me, part] = xs[me, part]

    position = lax.broadcasted_iota(jnp.int32, (n * width, 1), 0)
    valid = lax.rem(position, width) < lon_cols

    def finish_chunk(ch):
        for d in range(n - 1):
            back(ch, d).wait_recv()
        part = pl.ds(ch * chunk, chunk)
        for o in range(n):
            block = x_ref[pl.ds(o * rows_own + ch * chunk, chunk)].astype(F32)
            first = (block + ret[o, part].astype(F32)).astype(BF16).astype(F32)
            base = o * chunk * width
            start = pl.multiple_of(ch * (band * width) + base, chunk * width)
            first2 = first.reshape(chunk * width, features)
            second_norm = layer_norm(first2, gains[1:2])
            for half in range(halves):
                lanes = slice(half * LANES, (half + 1) * LANES)
                state[half, pl.ds(start, chunk * width), :] = first2[:, lanes]
                normed[half, pl.ds(base, chunk * width), :] = second_norm[:, lanes]
        rows = pl.ds(pl.multiple_of(ch * band, band), band)
        for c in range(lon_cols):
            for half in range(halves):
                lanes = slice(half * LANES, (half + 1) * LANES)
                column = normed.at[half][pl.ds(c, band, stride=width), :]
                lsend[c, rows, lanes] = column.astype(BF16)
        for d in range(m - 1):
            lat_forth(ch, d).start()
        lrecv[mine, :, rows, :] = lsend[pl.ds(mine * cols_own, cols_own), rows, :]

    @pl.loop(0, chunks)
    def _(ch):
        for d in range(n - 1):
            forth(ch, d).wait_recv()

        @pl.loop(0, chunk)
        def _(i):
            row = ch * chunk + i
            line = recv[:, row].reshape(n * width, features)
            mixed = attend(line, wqk1[...], wvt1[...], wo1[...], lambda h: scales[0, h], heads, valid)
            obuf[:, row] = mixed.reshape(n, width, features)

        for d in range(n - 1):
            back(ch, d).start()
        part = pl.ds(ch * chunk, chunk)
        ret[me, part] = obuf[me, part]

        @pl.when(ch > 0)
        def _():
            finish_chunk(ch - 1)

    finish_chunk(chunks - 1)

    @pl.loop(0, chunks)
    def _(ch):
        for d in range(m - 1):
            lat_forth(ch, d).wait_recv()

    @pl.loop(0, cols_own)
    def _(c):
        line = lrecv[:, c].reshape(m * lat_rows, features)
        mixed = attend(line, wqk2[...], wvt2[...], wo2[...], lambda h: scales[1, h], heads, None)
        lout[:, c] = mixed.reshape(m, lat_rows, features)
        for d in range(m - 1):
            lat_back(c, d).start()
        lret[mine * cols_own + c] = lout[mine, c]

    def add_column(col):
        place = pl.ds(col, lat_rows, stride=width)
        for half in range(halves):
            lanes = slice(half * LANES, (half + 1) * LANES)
            total = state.at[half][place, :] + lret[col, :, lanes].astype(F32)
            state.at[half][place, :] = total.astype(BF16).astype(F32)

    @pl.loop(0, cols_own)
    def _(c):
        add_column(mine * cols_own + c)

    @pl.loop(0, cols_own)
    def _(c):
        for d in range(m - 1):
            lat_back(c, d).wait_recv()
            source = lax.rem(mine + m - (d + 1), m)
            add_column(source * cols_own + c)

    @pl.loop(0, chunks)
    def _(ch):
        for o in range(n):
            start = pl.multiple_of(ch * (band * width) + o * chunk * width, chunk * width)
            for half in range(halves):
                lanes = slice(half * LANES, (half + 1) * LANES)
                block = state[half, pl.ds(start, chunk * width), :].astype(BF16)
                out_ref[pl.ds(o * rows_own + ch * chunk, chunk), :, lanes] = block.reshape(
                    chunk, width, LANES
                )
        for d in range(n - 1):
            forth(ch, d).wait_send()
            back(ch, d).wait_send()
        for d in range(m - 1):
            lat_forth(ch, d).wait_send()

    @pl.loop(0, cols_own)
    def _(c):
        for d in range(m - 1):
            lat_back(c, d).wait_send()


def chunk_of(rows_own, n):
    for size in range(4, rows_own + 1):
        if rows_own % size == 0 and (size * n) % 16 == 0:
            return size
    return rows_own


def attention(fields, norm_gains, lon_qkv, lon_out, lat_qkv, lat_out, logit_scales):
    lat_rows, lon_cols, features = fields.shape
    heads = logit_scales.shape[1]
    n, m = lax.axis_size("lon"), lax.axis_size("lat")
    width = -(-lon_cols // 16) * 16
    rows_own, cols_own = lat_rows // n, lon_cols // m
    chunk = chunk_of(rows_own, n)
    chunks, band = rows_own // chunk, chunk * n
    padded = jnp.pad(fields, ((0, 0), (0, width - lon_cols), (0, 0)))
    vmem = pl.BlockSpec(memory_space=pltpu.VMEM)
    dma = pltpu.SemaphoreType.DMA
    split = 2 * features
    return pl.pallas_call(
        functools.partial(attention_kernel, n, m, heads, lon_cols, chunk),
        out_shape=jax.ShapeDtypeStruct((lat_rows, width, features), BF16),
        in_specs=[vmem] * 8 + [pl.BlockSpec(memory_space=pltpu.SMEM)],
        out_specs=vmem,
        scratch_shapes=[
            pltpu.VMEM((n, rows_own, width, features), BF16),
            pltpu.VMEM((n, rows_own, width, features), BF16),
            pltpu.VMEM((n, rows_own, width, features), BF16),
            pltpu.VMEM((n, rows_own, width, features), BF16),
            pltpu.VMEM((features // LANES, band * width, LANES), F32),
            pltpu.VMEM((features // LANES, lat_rows * width, LANES), F32),
            pltpu.VMEM((lon_cols, lat_rows, features), BF16),
            pltpu.VMEM((m, cols_own, lat_rows, features), BF16),
            pltpu.VMEM((m, cols_own, lat_rows, features), BF16),
            pltpu.VMEM((lon_cols, lat_rows, features), BF16),
            dma((chunks, n - 1)), dma((chunks, n - 1)),
            dma((chunks, n - 1)), dma((chunks, n - 1)),
            dma((chunks, m - 1)), dma((chunks, m - 1)),
            dma((cols_own, m - 1)), dma((cols_own, m - 1)),
        ],
        compiler_params=pltpu.CompilerParams(
            collective_id=0, has_side_effects=True, vmem_limit_bytes=60 * 2**20
        ),
    )(
        padded, norm_gains,
        lon_qkv[:, :split], lon_qkv[:, split:].T, lon_out,
        lat_qkv[:, :split], lat_qkv[:, split:].T, lat_out,
        logit_scales,
    )


def mixer_kernel(rows, lon_cols, wide, taps, gains, w_in, w_down, out):
    step = pl.program_id(0)
    width, features = wide.shape[1], wide.shape[2]
    hidden_len = w_down.shape[0]
    margin = KERNEL // 2
    lines = wide[pl.ds(step * rows, rows + 2 * margin)].astype(F32)
    smoothed = None
    for dx in range(KERNEL):
        term = None
        for dy in range(KERNEL):
            tap = taps[pl.ds(dy * KERNEL + dx, 1), :][None]
            piece = tap * lines[dy : dy + rows]
            term = piece if term is None else term + piece
        if dx:
            term = pltpu.roll(term, width - dx, 1)
        smoothed = term if smoothed is None else smoothed + term
    normed = layer_norm(smoothed.reshape(rows * width, features), gains[2:3]).astype(BF16)
    gate_up = jnp.dot(normed, w_in[...], preferred_element_type=F32)
    half = gate_up[:, :hidden_len] * 0.5
    hidden = (half * (1.0 + jnp.tanh(half)) * gate_up[:, hidden_len:]).astype(BF16)
    update = jnp.dot(hidden, w_down[...], preferred_element_type=F32)
    centre = pltpu.roll(lines[margin : margin + rows], width - margin, 1)
    total = centre + update.reshape(rows, width, features)
    out[...] = total[:, :lon_cols].astype(BF16)


def mixer(second, conv_taps, norm_gains, mlp_in, mlp_down):
    lat_rows, lon_cols, features = second.shape
    margin = KERNEL // 2
    widened = extended(second, (("lon", 1),), margin, True)
    widened = extended(widened, (("lat", 0),), margin, False)
    width = -(-widened.shape[1] // 16) * 16
    widened = jnp.pad(widened, ((0, 0), (0, width - widened.shape[1]), (0, 0)))
    rows = next(r for r in (8, 6, 4, 3, 2, 1) if lat_rows % r == 0)
    vmem = pl.BlockSpec(memory_space=pltpu.VMEM)
    return pl.pallas_call(
        functools.partial(mixer_kernel, rows, lon_cols),
        grid=(lat_rows // rows,),
        out_shape=jax.ShapeDtypeStruct((lat_rows, lon_cols, features), BF16),
        in_specs=[vmem] * 5,
        out_specs=pl.BlockSpec((rows, lon_cols, features), lambda i: (i, 0, 0)),
        compiler_params=pltpu.CompilerParams(vmem_limit_bytes=48 * 2**20),
    )(widened, conv_taps, norm_gains, mlp_in, mlp_down)


def per_device(
    fields, norm_gains, lon_qkv, lon_out, lat_qkv, lat_out, logit_scales, conv_taps, mlp_in, mlp_down
):
    lon_cols = fields.shape[1]
    second = attention(fields, norm_gains, lon_qkv, lon_out, lat_qkv, lat_out, logit_scales)
    return mixer(second[:, :lon_cols], conv_taps, norm_gains, mlp_in, mlp_down)


def solution(mesh):
    in_specs = (P(("groups", "lat"), "lon", None), P(), P(), P(), P(), P(), P(), P(), P(), P())
    out_specs = P(("groups", "lat"), "lon", None)
    return jax.shard_map(
        per_device, mesh=mesh, in_specs=in_specs, out_specs=out_specs, check_vma=False
    )
```

time: 313 us -> 164 us (0.52)
  Pallas kernels: 0 us -> 134 us
  matrix products: 90.6 us -> 0 us
  blocking collectives: 57.4 us -> 0 us
  waiting for transfers between devices: 55.3 us -> 8.69 us
  other arithmetic: 42.3 us -> 1.96 us
  local copies, waits for them, and re-layouts: 44.8 us -> 10.4 us
  starting transfers between devices: 18.3 us -> 6.79 us
    pallas_call x0 -> x2, Pallas kernels: none -> 134 us  [the longest x1 117 us: attention(): pl.pallas_call(functools.partial(attention_kernel, n, m, heads, lon_cols,...]
    dot_general x38 -> x0, matrix products: 90.6 us -> none  [the longest x16 41 us: head_step(): jnp.einsum(EINSUM_FORMS[form][1], weights.astype(jnp.bfloat16), values_in...]
    all_to_all x2 -> x0, blocking collectives: 57.4 us -> none  [the longest x1 35.1 us: per_device(): lax.all_to_all(mixed_out.reshape(exchanged.shape), 'lon', split_axis=2, c...]
    all_to_all x2 -> x0, waiting for transfers between devices: 47 us -> none  [the longest x1 29.9 us: per_device(): lax.all_to_all(stacked, 'lon', split_axis=0, concat_axis=2, tiled=True)]
    reduce_sum x22 -> x0, other arithmetic: 27.7 us -> none  [the longest x16 12.5 us: head_step(): running_sum = running_sum * fading + jnp.sum(weights, -1)]
    slice x11 -> x6, local copies, waits for them, and re-layouts: 19.5 us -> 3.48 us  [the longest x1 1.79 us: attention(): lon_qkv[:, :split]]
    convert_element_type x10 -> x0, other arithmetic: 14.2 us -> none  [the longest x1 4.53 us: per_device(): return (second_state.astype(jnp.float32) + update).astype(jnp.bfloat16)]
    dynamic_slice x16 -> x0, local copies, waits for them, and re-layouts: 9.85 us -> none  [attend_heads(): return lax.map(one_head, (state, queries, keys_in, values_in, factors))]
  transfers between devices with their start and end apart: 6 -> 4, of which waited for: 5 -> 3; matrix products, arithmetic and copies ran while one was open for 0% -> 0% of each run, Pallas kernels for 0% -> 0%
where the time goes in v1:
time: 164 us; the launch traced here: 162 us
  Pallas kernels  134 us (82%)
  local copies, waits for them, and re-layouts  10.4 us (6%)
  waiting for transfers between devices  8.69 us (5%)
  starting transfers between devices  6.79 us (4%)
  other arithmetic  1.96 us (1%)
    pallas_call x1, Pallas kernels, attention(): pl.pallas_call(functools.partial(attention_kernel, n, m, heads, lon_cols,...  117 us
    pallas_call x1, Pallas kernels, mixer(): pl.pallas_call(functools.partial(mixer_kernel, rows, lon_cols), grid=(lat...  17.1 us
    ppermute x2, waiting for transfers between devices, extended(): after = lax.ppermute(leading, axis, down)  5.79 us
    ppermute x2, starting transfers between devices, extended(): before = lax.ppermute(last, axis, up)  3.78 us
  transfers between devices with their start and end apart: 4, of which 3 were waited for; matrix products, arithmetic and copies ran while one was open for 0% of the time, Pallas kernels for 0%

profile of v1, /device:TPU:25, one launch (start us, length us, event | category | flops | bytes accessed | tf_op | source)
XLA Modules:
  0.0 161.7 jit_solution(15474477772206446847)
XLA Ops:
  0.0 1.8 %slice.29.wqk1 = bf16[256,512]{1,0:T(8,128)(2,1)} slice(bf16[256,768]{1,0:T(8,128)(2,1)} %param.12), slice={[0:256], [0:512]} | slice | bytes 524288 | tf_op jit(solution)/shard_map/slice | solution.py:286
  1.8 1.7 %slice.31.wqk2 = bf16[256,512]{1,0:T(8,128)(2,1)} slice(bf16[256,768]{1,0:T(8,128)(2,1)} %param.14), slice={[0:256], [0:512]} | slice | bytes 524288 | tf_op jit(solution)/shard_map/slice | solution.py:287
  3.5 0.7 copy.15
  4.2 0.8 copy.16
  5.0 0.8 copy.11
  5.8 1.4 pad.4.x_ref
  7.1 116.6 %shard_map.100 = bf16[96,32,256]{2,1,0:T(8,128)(2,1)} custom-call(bf16[96,32,256]{2,1,0:T(8,128)(2,1)} %pad.4.x_ref, f32[3,256]{1,0:T(4,128)} %gains.3, bf16[256,512]{1,0:T(8,128)(2,1)} %slice.29.wqk1, bf16[256,256]{1,0:T(8,128)(2,1)} %bitcast.5, bf16[256,256]{1,0:T(8,128)(2,1)} %wo1.1, bf16[256,512]{1,0:T(8,128)(2,1)} %slice.31.wqk2, ...), custom_call_target="tpu_custom_call" | custom-call | tf_op jit(solution)/shard_map/pallas_call | solution.py:260
  123.8 1.4 fusion
  125.2 0.6 collective-permute-start
  125.7 1.0 collective-permute-start.1
  126.7 2.9 %collective-permute-done = bf16[96,2,256]{2,1,0:T(2,128)(2,1)S(1)} collective-permute-done((bf16[96,2,256]{2,1,0:T(2,128)(2,1)S(1)}, bf16[96,2,256]{2,1,0:T(2,128)(2,1)S(1)}, u32[]{:S(2)}, u32[]{:S(2)}) %collective-permute-start) | collective-permute-done | bytes 98336 | tf_op jit(solution)/shard_map/ppermute | solution.py:27
  129.6 2.5 %collective-permute-done.1 = bf16[96,2,256]{2,1,0:T(2,128)(2,1)S(1)} collective-permute-done((bf16[96,2,256]{2,1,0:T(2,128)(2,1)S(1)}, bf16[96,2,256]{2,1,0:T(2,128)(2,1)S(1)}, u32[]{:S(2)}, u32[]{:S(2)}) %collective-permute-start.1) | collective-permute-done | bytes 98336 | tf_op jit(solution)/shard_map/ppermute | solution.py:28
  132.1 0.8 pad_maximum_fusion.3
  132.9 3.2 %collective-permute-start.2 = (bf16[2,32,256]{2,1,0:T(8,128)(2,1)S(1)}, bf16[2,32,256]{2,1,0:T(8,128)(2,1)S(1)}, u32[]{:S(2)}, u32[]{:S(2)}) collective-permute-start(bf16[2,32,256]{2,1,0:T(8,128)(2,1)S(1)} %get-tuple-element.5), channel_id=1, source_target_pairs={{0,1},{1,2},{2,3},{4,5},{5,6},{6,7},{8,9},{9,10},{10,11},{12,13},{... | collective-permute-start | bytes 98312 | tf_op jit(solution)/shard_map/ppermute | solution.py:27
  136.1 0.0 copy-start
  136.1 0.0 copy-start.1
  136.1 0.0 copy-start.2
  136.1 0.0 copy-start.3
  136.2 2.1 %collective-permute-start.3 = (bf16[2,32,256]{2,1,0:T(8,128)(2,1)S(1)}, bf16[2,32,256]{2,1,0:T(8,128)(2,1)S(1)}, u32[]{:S(2)}, u32[]{:S(2)}) collective-permute-start(bf16[2,32,256]{2,1,0:T(8,128)(2,1)S(1)} %get-tuple-element.6), channel_id=1, source_target_pairs={{1,0},{2,1},{3,2},{5,4},{6,5},{7,6},{9,8},{10,9},{11,10},{13,12},{... | collective-permute-start | bytes 98312 | tf_op jit(solution)/shard_map/ppermute | solution.py:28
  138.2 0.0 collective-permute-done.2
  138.2 3.3 %collective-permute-done.3 = bf16[2,32,256]{2,1,0:T(8,128)(2,1)S(1)} collective-permute-done((bf16[2,32,256]{2,1,0:T(8,128)(2,1)S(1)}, bf16[2,32,256]{2,1,0:T(8,128)(2,1)S(1)}, u32[]{:S(2)}, u32[]{:S(2)}) %collective-permute-start.3) | collective-permute-done | bytes 32800 | tf_op jit(solution)/shard_map/ppermute | solution.py:28
  141.5 1.2 pad_maximum_fusion.wide
  142.7 17.1 %shard_map.101 = bf16[96,28,256]{2,1,0:T(8,128)(2,1)S(1)} custom-call(bf16[100,32,256]{2,1,0:T(8,128)(2,1)S(1)} %pad_maximum_fusion.wide, f32[25,256]{1,0:T(8,128)S(1)} %copy-done.2, f32[3,256]{1,0:T(4,128)S(1)} %copy-done.3, bf16[256,2048]{1,0:T(8,128)(2,1)S(1)} %copy-done, bf16[1024,256]{1,0:T(8,128)(2,1)S(1)} %copy-done.1), custom_call_target="tpu_custom_call" | custom-call | tf_op jit(solution)/shard_map/pallas_call | solution.py:327
  159.8 1.8 %copy.14 = bf16[96,28,256]{2,0,1:T(8,128)(2,1)} copy(bf16[96,28,256]{2,1,0:T(8,128)(2,1)S(1)} %shard_map.101) | data formatting | bytes 2752512 | tf_op jit(solution)/shard_map/pallas_call | solution.py:327
  (12 shorter events, 0.0 us)
Async XLA Ops:
  0.0 3.5 %slice-start = ((bf16[256,768]{1,0:T(8,128)(2,1)}), bf16[256,256]{1,0:T(8,128)(2,1)S(1)}, s32[]{:S(2)}) async-start(bf16[256,768]{1,0:T(8,128)(2,1)} %param.12), calls=%async_computation | async-start | bytes 262144 | tf_op jit(solution)/shard_map/slice | solution.py:286
  0.0 4.2 %slice-start.1 = ((bf16[256,768]{1,0:T(8,128)(2,1)}), bf16[256,256]{1,0:T(8,128)(2,1)S(1)}, s32[]{:S(2)}) async-start(bf16[256,768]{1,0:T(8,128)(2,1)} %param.14), calls=%async_computation.1 | async-start | bytes 262144 | tf_op jit(solution)/shard_map/slice | solution.py:287
  0.0 5.0 %copy-start.5 = (bf16[96,28,256]{2,0,1:T(8,128)(2,1)S(1)}, bf16[96,28,256]{2,0,1:T(8,128)(2,1)}, u32[]{:S(2)}) copy-start(bf16[96,28,256]{2,0,1:T(8,128)(2,1)} %param.10) | copy-start | bytes 4128772
  123.7 17.8 %copy-start.4 = (bf16[96,32,256]{2,1,0:T(8,128)(2,1)S(1)}, bf16[96,32,256]{2,1,0:T(8,128)(2,1)}, u32[]{:S(2)}) copy-start(bf16[96,32,256]{2,1,0:T(8,128)(2,1)} %shard_map.100) | copy-start | bytes 4718596
  125.2 4.4 %collective-permute-start = (bf16[96,2,256]{2,1,0:T(2,128)(2,1)S(1)}, bf16[96,2,256]{2,1,0:T(2,128)(2,1)S(1)}, u32[]{:S(2)}, u32[]{:S(2)}) collective-permute-start(bf16[96,2,256]{2,1,0:T(2,128)(2,1)S(1)} %get-tuple-element.7), channel_id=1, source_target_pairs={{0,4},{4,8},{8,12},{12,0},{1,5},{5,9},{9,13},{13,1},{2,6},{6,10},{... | collective-permute-start | bytes 294920 | tf_op jit(solution)/shard_map/ppermute | solution.py:27
  125.7 6.4 %collective-permute-start.1 = (bf16[96,2,256]{2,1,0:T(2,128)(2,1)S(1)}, bf16[96,2,256]{2,1,0:T(2,128)(2,1)S(1)}, u32[]{:S(2)}, u32[]{:S(2)}) collective-permute-start(bf16[96,2,256]{2,1,0:T(2,128)(2,1)S(1)} %get-tuple-element.8), channel_id=1, source_target_pairs={{4,0},{8,4},{12,8},{0,12},{5,1},{9,5},{13,9},{1,13},{6,2},{10,6},{... | collective-permute-start | bytes 294920 | tf_op jit(solution)/shard_map/ppermute | solution.py:28
  132.9 5.3 %collective-permute-start.2 = (bf16[2,32,256]{2,1,0:T(8,128)(2,1)S(1)}, bf16[2,32,256]{2,1,0:T(8,128)(2,1)S(1)}, u32[]{:S(2)}, u32[]{:S(2)}) collective-permute-start(bf16[2,32,256]{2,1,0:T(8,128)(2,1)S(1)} %get-tuple-element.5), channel_id=1, source_target_pairs={{0,1},{1,2},{2,3},{4,5},{5,6},{6,7},{8,9},{9,10},{10,11},{12,13},{... | collective-permute-start | bytes 98312 | tf_op jit(solution)/shard_map/ppermute | solution.py:27
  136.1 6.6 %copy-start = (bf16[256,2048]{1,0:T(8,128)(2,1)S(1)}, bf16[256,2048]{1,0:T(8,128)(2,1)}, u32[]{:S(2)}) copy-start(bf16[256,2048]{1,0:T(8,128)(2,1)} %w_in.1) | copy-start | bytes 3145732
  136.1 6.6 %copy-start.1 = (bf16[1024,256]{1,0:T(8,128)(2,1)S(1)}, bf16[1024,256]{1,0:T(8,128)(2,1)}, u32[]{:S(2)}) copy-start(bf16[1024,256]{1,0:T(8,128)(2,1)} %w_down.1) | copy-start | bytes 1572868
  136.1 6.6 %copy-start.2 = (f32[25,256]{1,0:T(8,128)S(1)}, f32[25,256]{1,0:T(8,128)}, u32[]{:S(2)}) copy-start(f32[25,256]{1,0:T(8,128)} %taps.1) | copy-start | bytes 76804
  136.1 6.6 %copy-start.3 = (f32[3,256]{1,0:T(4,128)S(1)}, f32[3,256]{1,0:T(4,128)}, u32[]{:S(2)}) copy-start(f32[3,256]{1,0:T(4,128)} %gains.3) | copy-start | bytes 9220
  136.2 5.4 %collective-permute-start.3 = (bf16[2,32,256]{2,1,0:T(8,128)(2,1)S(1)}, bf16[2,32,256]{2,1,0:T(8,128)(2,1)S(1)}, u32[]{:S(2)}, u32[]{:S(2)}) collective-permute-start(bf16[2,32,256]{2,1,0:T(8,128)(2,1)S(1)} %get-tuple-element.6), channel_id=1, source_target_pairs={{1,0},{2,1},{3,2},{5,4},{6,5},{7,6},{9,8},{10,9},{11,10},{13,12},{... | collective-permute-start | bytes 98312 | tf_op jit(solution)/shard_map/ppermute | solution.py:28

commit v2 on v1

v2 whole, which is shorter than its diff:
```python
import functools
import math

import jax
import jax.numpy as jnp
from jax import lax
from jax.experimental import pallas as pl
from jax.experimental.pallas import tpu as pltpu
from jax.sharding import PartitionSpec as P

KERNEL = 5
LANES = 128
EPSILON = 1e-05
MESH = pl.DeviceIdType.MESH
F32, BF16 = jnp.float32, jnp.bfloat16
NT = (((1,), (1,)), ((), ()))
TN = (((0,), (0,)), ((), ()))


def extended(x, sides, width, wrap):
    for axis, dim in sides:
        count, length = (lax.axis_size(axis), x.shape[dim])
        up = [(i, (i + 1) % count) for i in range(count if wrap else count - 1)]
        down = [(j, i) for i, j in up]
        last = lax.slice_in_dim(x, length - width, length, axis=dim)
        leading = lax.slice_in_dim(x, 0, width, axis=dim)
        before = lax.ppermute(last, axis, up)
        after = lax.ppermute(leading, axis, down)
        x = jnp.concatenate([before, x, after], axis=dim)
    return x


def layer_norm(values, gains):
    average = jnp.mean(values, -1, keepdims=True)
    centred = values - average
    spread = jnp.mean(centred * centred, -1, keepdims=True)
    return centred * lax.rsqrt(spread + EPSILON) * gains


def attend(x, wqk, wvt, wout, factor_of, heads, valid):
    features = x.shape[-1]
    size = features // heads
    qk = jnp.dot(x, wqk, preferred_element_type=F32).astype(BF16)
    queries, keys = qk[:, :features], qk[:, features:]
    values = lax.dot_general(wvt, x, NT, preferred_element_type=F32).astype(BF16)
    lane = lax.broadcasted_iota(jnp.int32, (1, features), 1) // size
    parts = []
    for h in range(heads):
        own = keys * (lane == h).astype(F32).astype(BF16)
        scores = lax.dot_general(own, queries, NT, preferred_element_type=F32)
        if valid is not None:
            scores = jnp.where(valid, scores, -1e30)
        top = jnp.max(scores, 0, keepdims=True)
        weights = jnp.exp2((scores - top) * (factor_of(h) * math.log2(math.e)))
        total = jnp.sum(weights, 0, keepdims=True)
        part = jnp.dot(
            values[h * size : (h + 1) * size], weights.astype(BF16), preferred_element_type=F32
        )
        parts.append(part / total)
    context = jnp.concatenate(parts, 0).astype(BF16)
    return lax.dot_general(context, wout, TN, preferred_element_type=F32)


def attention_kernel(
    n, m, heads, lon_cols, chunk,
    x_ref, gains, wqkv1, wo1, wqkv2, wo2, scales,
    out_ref,
    xs, recv, wide, mixed, obuf, ret, state, lsend, lrecv, lout, lret, wvt1, wvt2,
    fs, fr, bs, br, gs, gr, hs, hr,
):
    rows_own = xs.shape[1]
    width, features = xs.shape[2], xs.shape[3]
    chunks = rows_own // chunk
    lat_rows = rows_own * n
    cols_own = lon_cols // m
    halves = features // LANES
    split = 2 * features
    segment = obuf.shape[2]
    me = lax.axis_index("lon")
    mine = lax.axis_index("lat")
    lon_peers = [lax.rem(me + d, n) for d in range(1, n)]
    lat_peers = [lax.rem(mine + d, m) for d in range(1, m)]

    barrier = pltpu.get_barrier_semaphore()
    for peer in lon_peers:
        pl.semaphore_signal(barrier, inc=1, device_id={"lon": peer}, device_id_type=MESH)
    for peer in lat_peers:
        pl.semaphore_signal(barrier, inc=1, device_id={"lat": peer}, device_id_type=MESH)
    pl.semaphore_wait(barrier, n + m - 2)

    def forth(ch, d):
        peer = lon_peers[d]
        part = pl.ds(ch * chunk, chunk)
        return pltpu.make_async_remote_copy(
            src_ref=xs.at[peer, part], dst_ref=recv.at[me, part],
            send_sem=fs.at[ch, d], recv_sem=fr.at[ch, d],
            device_id={"lon": peer}, device_id_type=MESH,
        )

    def back(c, d):
        peer = lon_peers[d]
        return pltpu.make_async_remote_copy(
            src_ref=obuf.at[peer, c], dst_ref=ret.at[me, c],
            send_sem=bs.at[c, d], recv_sem=br.at[c, d],
            device_id={"lon": peer}, device_id_type=MESH,
        )

    def lat_forth(c, d):
        peer = lat_peers[d]
        return pltpu.make_async_remote_copy(
            src_ref=lsend.at[peer, c], dst_ref=lrecv.at[mine, c],
            send_sem=gs.at[c, d], recv_sem=gr.at[c, d],
            device_id={"lat": peer}, device_id_type=MESH,
        )

    def lat_back(c, d):
        peer = lat_peers[d]
        return pltpu.make_async_remote_copy(
            src_ref=lout.at[peer, c], dst_ref=lret.at[mine, c],
            send_sem=hs.at[c, d], recv_sem=hr.at[c, d],
            device_id={"lat": peer}, device_id_type=MESH,
        )

    @pl.loop(0, chunks)
    def _(ch):
        part = pl.ds(ch * chunk, chunk)
        for o in range(n):
            first_row = o * rows_own + ch * chunk
            block = x_ref[pl.ds(first_row, chunk)].astype(F32)
            xs[o, part] = layer_norm(block, gains[0:1][None]).astype(BF16)
        for d in range(n - 1):
            forth(ch, d).start()
        recv[me, part] = xs[me, part]

    wvt1[...] = wqkv1[:, split:].astype(F32).T.astype(BF16)
    wvt2[...] = wqkv2[:, split:].astype(F32).T.astype(BF16)

    @pl.loop(0, lat_rows // chunk)
    def _(i):
        block = x_ref[pl.ds(i * chunk, chunk)].astype(F32).reshape(chunk * width, features)
        place = pl.ds(pl.multiple_of(i * (chunk * width), chunk * width), chunk * width)
        for half in range(halves):
            wide[half, place, :] = block[:, half * LANES : (half + 1) * LANES]

    @pl.loop(0, cols_own)
    def _(c):
        for p in range(m):
            for half in range(halves):
                place = pl.ds(p * cols_own + c, lat_rows, stride=width)
                state[c, p, :, half * LANES : (half + 1) * LANES] = wide.at[half][place, :]

    position = lax.broadcasted_iota(jnp.int32, (n * width, 1), 0)
    valid = lax.rem(position, width) < lon_cols

    @pl.loop(0, chunks)
    def _(ch):
        for d in range(n - 1):
            forth(ch, d).wait_recv()

        @pl.loop(0, chunk)
        def _(i):
            row = ch * chunk + i
            line = recv[:, row].reshape(n * width, features)
            result = attend(
                line, wqkv1[:, :split], wvt1[...], wo1[...], lambda h: scales[0, h], heads, valid
            )
            place = pl.ds(row, n * width, stride=rows_own)
            for half in range(halves):
                mixed.at[half][place, :] = result[:, half * LANES : (half + 1) * LANES]

    spare = segment - m * rows_own

    @pl.loop(0, cols_own)
    def _(c):
        for j in range(n):
            for half in range(halves):
                pieces = []
                for p in range(m):
                    start = (j * width + p * cols_own + c) * rows_own
                    if rows_own % 8 == 0:
                        start = pl.multiple_of(start, 8)
                    pieces.append(mixed[half, pl.ds(start, rows_own), :])
                if spare:
                    pieces.append(jnp.zeros((spare, LANES), F32))
                block = jnp.concatenate(pieces, 0).astype(BF16)
                obuf[j, c, :, half * LANES : (half + 1) * LANES] = block
        for d in range(n - 1):
            back(c, d).start()
        ret[me, c] = obuf[me, c]

    def finish_lon(c):
        for d in range(n - 1):
            back(c, d).wait_recv()
        arrived = [ret[o, c].astype(F32) for o in range(n)]
        for p in range(m):
            lon_mix = jnp.concatenate(
                [block[p * rows_own : (p + 1) * rows_own] for block in arrived], 0
            )
            first = (state[c, p] + lon_mix).astype(BF16).astype(F32)
            state[c, p] = first
            lsend[p, c] = layer_norm(first, gains[1:2]).astype(BF16)
        for d in range(m - 1):
            lat_forth(c, d).start()
        lrecv[mine, c] = lsend[mine, c]

    def lat_line(c):
        for d in range(m - 1):
            lat_forth(c, d).wait_recv()
        line = lrecv[:, c].reshape(m * lat_rows, features)
        result = attend(
            line, wqkv2[:, :split], wvt2[...], wo2[...], lambda h: scales[1, h], heads, None
        )
        lout[:, c] = result.astype(BF16).reshape(m, lat_rows, features)
        for d in range(m - 1):
            lat_back(c, d).start()
        lret[mine, c] = lout[mine, c]

    def finish_lat(c):
        for d in range(m - 1):
            lat_back(c, d).wait_recv()
        for p in range(m):
            total = (state[c, p] + lret[p, c].astype(F32)).astype(BF16).astype(F32)
            place = pl.ds(p * cols_own + c, lat_rows, stride=width)
            for half in range(halves):
                wide.at[half][place, :] = total[:, half * LANES : (half + 1) * LANES]

    finish_lon(0)

    @pl.loop(0, cols_own)
    def _(c):
        @pl.when(c < cols_own - 1)
        def _():
            finish_lon(c + 1)

        lat_line(c)

        @pl.when(c > 0)
        def _():
            finish_lat(c - 1)

    finish_lat(cols_own - 1)

    @pl.loop(0, lat_rows // chunk)
    def _(i):
        place = pl.ds(pl.multiple_of(i * (chunk * width), chunk * width), chunk * width)
        for half in range(halves):
            block = wide[half, place, :].astype(BF16).reshape(chunk, width, LANES)
            out_ref[pl.ds(i * chunk, chunk), :, half * LANES : (half + 1) * LANES] = block

    @pl.loop(0, chunks)
    def _(ch):
        for d in range(n - 1):
            forth(ch, d).wait_send()

    @pl.loop(0, cols_own)
    def _(c):
        for d in range(n - 1):
            back(c, d).wait_send()
        for d in range(m - 1):
            lat_forth(c, d).wait_send()
            lat_back(c, d).wait_send()


def attention(fields, norm_gains, lon_qkv, lon_out, lat_qkv, lat_out, logit_scales):
    lat_rows, lon_cols, features = fields.shape
    heads = logit_scales.shape[1]
    n, m = lax.axis_size("lon"), lax.axis_size("lat")
    width = -(-lon_cols // 16) * 16
    rows_own, cols_own = lat_rows // n, lon_cols // m
    chunk = next(size for size in (4, 3, 2, 1) if rows_own % size == 0)
    chunks, halves = rows_own // chunk, features // LANES
    segment = -(-(m * rows_own) // 16) * 16
    padded = jnp.pad(fields, ((0, 0), (0, width - lon_cols), (0, 0)))
    vmem = pl.BlockSpec(memory_space=pltpu.VMEM)
    dma = pltpu.SemaphoreType.DMA
    return pl.pallas_call(
        functools.partial(attention_kernel, n, m, heads, lon_cols, chunk),
        out_shape=jax.ShapeDtypeStruct((lat_rows, width, features), BF16),
        in_specs=[vmem] * 6 + [pl.BlockSpec(memory_space=pltpu.SMEM)],
        out_specs=vmem,
        scratch_shapes=[
            pltpu.VMEM((n, rows_own, width, features), BF16),
            pltpu.VMEM((n, rows_own, width, features), BF16),
            pltpu.VMEM((halves, lat_rows * width, LANES), F32),
            pltpu.VMEM((halves, n * width * rows_own, LANES), F32),
            pltpu.VMEM((n, cols_own, segment, features), BF16),
            pltpu.VMEM((n, cols_own, segment, features), BF16),
            pltpu.VMEM((cols_own, m, lat_rows, features), F32),
            pltpu.VMEM((m, cols_own, lat_rows, features), BF16),
            pltpu.VMEM((m, cols_own, lat_rows, features), BF16),
            pltpu.VMEM((m, cols_own, lat_rows, features), BF16),
            pltpu.VMEM((m, cols_own, lat_rows, features), BF16),
            pltpu.VMEM((features, features), BF16),
            pltpu.VMEM((features, features), BF16),
            dma((chunks, n - 1)), dma((chunks, n - 1)),
            dma((cols_own, n - 1)), dma((cols_own, n - 1)),
            dma((cols_own, m - 1)), dma((cols_own, m - 1)),
            dma((cols_own, m - 1)), dma((cols_own, m - 1)),
        ],
        compiler_params=pltpu.CompilerParams(
            collective_id=0, has_side_effects=True, vmem_limit_bytes=60 * 2**20
        ),
    )(padded, norm_gains, lon_qkv, lon_out, lat_qkv, lat_out, logit_scales)


def mixer_kernel(rows, lon_cols, wide, taps, gains, w_in, w_down, out):
    step = pl.program_id(0)
    width, features = wide.shape[1], wide.shape[2]
    hidden_len = w_down.shape[0]
    margin = KERNEL // 2
    lines = wide[pl.ds(step * rows, rows + 2 * margin)].astype(F32)
    smoothed = None
    for dx in range(KERNEL):
        term = None
        for dy in range(KERNEL):
            tap = taps[pl.ds(dy * KERNEL + dx, 1), :][None]
            piece = tap * lines[dy : dy + rows]
            term = piece if term is None else term + piece
        if dx:
            term = pltpu.roll(term, width - dx, 1)
        smoothed = term if smoothed is None else smoothed + term
    normed = layer_norm(smoothed.reshape(rows * width, features), gains[2:3]).astype(BF16)
    gate_up = jnp.dot(normed, w_in[...], preferred_element_type=F32)
    half = gate_up[:, :hidden_len] * 0.5
    hidden = (half * (1.0 + jnp.tanh(half)) * gate_up[:, hidden_len:]).astype(BF16)
    update = jnp.dot(hidden, w_down[...], preferred_element_type=F32)
    centre = pltpu.roll(lines[margin : margin + rows], width - margin, 1)
    total = centre + update.reshape(rows, width, features)
    out[...] = total[:, :lon_cols].astype(BF16)


def mixer(second, conv_taps, norm_gains, mlp_in, mlp_down):
    lat_rows, lon_cols, features = second.shape
    margin = KERNEL // 2
    widened = extended(second, (("lon", 1),), margin, True)
    widened = extended(widened, (("lat", 0),), margin, False)
    width = -(-widened.shape[1] // 16) * 16
    widened = jnp.pad(widened, ((0, 0), (0, width - widened.shape[1]), (0, 0)))
    rows = next(r for r in (8, 6, 4, 3, 2, 1) if lat_rows % r == 0)
    vmem = pl.BlockSpec(memory_space=pltpu.VMEM)
    return pl.pallas_call(
        functools.partial(mixer_kernel, rows, lon_cols),
        grid=(lat_rows // rows,),
        out_shape=jax.ShapeDtypeStruct((lat_rows, lon_cols, features), BF16),
        in_specs=[vmem] * 5,
        out_specs=pl.BlockSpec((rows, lon_cols, features), lambda i: (i, 0, 0)),
        compiler_params=pltpu.CompilerParams(vmem_limit_bytes=48 * 2**20),
    )(widened, conv_taps, norm_gains, mlp_in, mlp_down)


def per_device(
    fields, norm_gains, lon_qkv, lon_out, lat_qkv, lat_out, logit_scales, conv_taps, mlp_in, mlp_down
):
    lon_cols = fields.shape[1]
    second = attention(fields, norm_gains, lon_qkv, lon_out, lat_qkv, lat_out, logit_scales)
    return mixer(second[:, :lon_cols], conv_taps, norm_gains, mlp_in, mlp_down)


def solution(mesh):
    in_specs = (P(("groups", "lat"), "lon", None), P(), P(), P(), P(), P(), P(), P(), P(), P())
    out_specs = P(("groups", "lat"), "lon", None)
    return jax.shard_map(
        per_device, mesh=mesh, in_specs=in_specs, out_specs=out_specs, check_vma=False
    )
```

time: 164 us -> 151 us (0.921); the launches traced: 162 us -> 150 us
  Pallas kernels: 134 us -> 126 us
  local copies, waits for them, and re-layouts: 10.4 us -> 6.73 us
    pallas_call x1, Pallas kernels: 117 us -> 109 us  [attention(): pl.pallas_call(functools.partial(attention_kernel, n, m, heads, lon_cols,...]
    slice x6 -> x0, local copies, waits for them, and re-layouts: 3.48 us -> none  [the longest x1 1.79 us: attention(): lon_qkv[:, :split]]
where the time goes in v2:
time: 151 us; the launch traced here: 150 us
  Pallas kernels  126 us (83%)
  waiting for transfers between devices  8.24 us (5%)
  starting transfers between devices  7.34 us (5%)
  local copies, waits for them, and re-layouts  6.73 us (4%)
  other arithmetic  1.96 us (1%)
    pallas_call x1, Pallas kernels, attention(): pl.pallas_call(functools.partial(attention_kernel, n, m, heads, lon_cols,...  109 us
    pallas_call x1, Pallas kernels, mixer(): pl.pallas_call(functools.partial(mixer_kernel, rows, lon_cols), grid=(lat...  17.1 us
    ppermute x2, waiting for transfers between devices, extended(): after = lax.ppermute(leading, axis, down)  5.16 us
    ppermute x2, starting transfers between devices, extended(): before = lax.ppermute(last, axis, up)  3.82 us
    ppermute x2, starting transfers between devices, extended(): after = lax.ppermute(leading, axis, down)  3.52 us
    ppermute x2, waiting for transfers between devices, extended(): before = lax.ppermute(last, axis, up)  3.08 us
  transfers between devices with their start and end apart: 4, of which 3 were waited for; matrix products, arithmetic and copies ran while one was open for 0% of the time, Pallas kernels for 0%

profile of v2, /device:TPU:25, one launch (start us, length us, event | category | flops | bytes accessed | tf_op | source)
XLA Modules:
  0.0 150.3 jit_solution(7190166643029516245)
XLA Ops:
  0.0 2.1 %copy.11 = bf16[96,28,256]{2,1,0:T(8,128)(2,1)S(1)} copy(bf16[96,28,256]{2,0,1:T(8,128)(2,1)} %param.10) | data formatting | bytes 2752512 | tf_op args[0]
  2.1 1.3 pad.4.x_ref
  3.5 108.8 %shard_map.100 = bf16[96,32,256]{2,1,0:T(8,128)(2,1)} custom-call(bf16[96,32,256]{2,1,0:T(8,128)(2,1)} %pad.4.x_ref, f32[3,256]{1,0:T(4,128)} %gains.3, bf16[256,768]{1,0:T(8,128)(2,1)} %wqkv1.1, bf16[256,256]{1,0:T(8,128)(2,1)} %wo1.1, bf16[256,768]{1,0:T(8,128)(2,1)} %wqkv2.1, bf16[256,256]{1,0:T(8,128)(2,1)} %wo2.1, f32[2,8]{1,0:T(2,128)} %scales.1), custom_call_target="tpu_custom_call" | custom-call | tf_op jit(solution)/shard_map/pallas_call | solution.py:276
  112.3 0.0 copy-start.4
  112.3 1.4 fusion
  113.7 0.1 collective-permute-start
  113.8 1.5 collective-permute-start.1
  115.3 3.1 %collective-permute-done = bf16[96,2,256]{2,1,0:T(2,128)(2,1)S(1)} collective-permute-done((bf16[96,2,256]{2,1,0:T(2,128)(2,1)S(1)}, bf16[96,2,256]{2,1,0:T(2,128)(2,1)S(1)}, u32[]{:S(2)}, u32[]{:S(2)}) %collective-permute-start) | collective-permute-done | bytes 98336 | tf_op jit(solution)/shard_map/ppermute | solution.py:27
  118.3 1.9 %collective-permute-done.1 = bf16[96,2,256]{2,1,0:T(2,128)(2,1)S(1)} collective-permute-done((bf16[96,2,256]{2,1,0:T(2,128)(2,1)S(1)}, bf16[96,2,256]{2,1,0:T(2,128)(2,1)S(1)}, u32[]{:S(2)}, u32[]{:S(2)}) %collective-permute-start.1) | collective-permute-done | bytes 98336 | tf_op jit(solution)/shard_map/ppermute | solution.py:28
  120.2 0.8 pad_maximum_fusion.3
  121.0 3.8 %collective-permute-start.2 = (bf16[2,32,256]{2,1,0:T(8,128)(2,1)S(1)}, bf16[2,32,256]{2,1,0:T(8,128)(2,1)S(1)}, u32[]{:S(2)}, u32[]{:S(2)}) collective-permute-start(bf16[2,32,256]{2,1,0:T(8,128)(2,1)S(1)} %get-tuple-element.5), channel_id=1, source_target_pairs={{0,1},{1,2},{2,3},{4,5},{5,6},{6,7},{8,9},{9,10},{10,11},{12,13},{... | collective-permute-start | bytes 98312 | tf_op jit(solution)/shard_map/ppermute | solution.py:27
  124.8 0.0 copy-start
  124.8 0.0 copy-start.1
  124.8 0.0 copy-start.2
  124.8 0.0 copy-start.3
  124.8 2.1 %collective-permute-start.3 = (bf16[2,32,256]{2,1,0:T(8,128)(2,1)S(1)}, bf16[2,32,256]{2,1,0:T(8,128)(2,1)S(1)}, u32[]{:S(2)}, u32[]{:S(2)}) collective-permute-start(bf16[2,32,256]{2,1,0:T(8,128)(2,1)S(1)} %get-tuple-element.6), channel_id=1, source_target_pairs={{1,0},{2,1},{3,2},{5,4},{6,5},{7,6},{9,8},{10,9},{11,10},{13,12},{... | collective-permute-start | bytes 98312 | tf_op jit(solution)/shard_map/ppermute | solution.py:28
  126.9 0.0 collective-permute-done.2
  126.9 3.3 %collective-permute-done.3 = bf16[2,32,256]{2,1,0:T(8,128)(2,1)S(1)} collective-permute-done((bf16[2,32,256]{2,1,0:T(8,128)(2,1)S(1)}, bf16[2,32,256]{2,1,0:T(8,128)(2,1)S(1)}, u32[]{:S(2)}, u32[]{:S(2)}) %collective-permute-start.3) | collective-permute-done | bytes 32800 | tf_op jit(solution)/shard_map/ppermute | solution.py:28
  130.2 0.0 copy-done.4
  130.2 1.2 pad_maximum_fusion.wide
  131.3 0.0 copy-done
  131.3 0.0 copy-done.1
  131.4 17.1 %shard_map.101 = bf16[96,28,256]{2,1,0:T(8,128)(2,1)S(1)} custom-call(bf16[100,32,256]{2,1,0:T(8,128)(2,1)S(1)} %pad_maximum_fusion.wide, f32[25,256]{1,0:T(8,128)S(1)} %copy-done.2, f32[3,256]{1,0:T(4,128)S(1)} %copy-done.3, bf16[256,2048]{1,0:T(8,128)(2,1)S(1)} %copy-done, bf16[1024,256]{1,0:T(8,128)(2,1)S(1)} %copy-done.1), custom_call_target="tpu_custom_call" | custom-call | tf_op jit(solution)/shard_map/pallas_call | solution.py:341
  148.5 1.8 %copy.12 = bf16[96,28,256]{2,0,1:T(8,128)(2,1)} copy(bf16[96,28,256]{2,1,0:T(8,128)(2,1)S(1)} %shard_map.101) | data formatting | bytes 2752512 | tf_op jit(solution)/shard_map/pallas_call | solution.py:341
  (2 shorter events, 0.0 us)
Async XLA Ops:
  112.3 17.9 %copy-start.4 = (bf16[96,32,256]{2,1,0:T(8,128)(2,1)S(1)}, bf16[96,32,256]{2,1,0:T(8,128)(2,1)}, u32[]{:S(2)}) copy-start(bf16[96,32,256]{2,1,0:T(8,128)(2,1)} %shard_map.100) | copy-start | bytes 4718596
  113.7 4.6 %collective-permute-start = (bf16[96,2,256]{2,1,0:T(2,128)(2,1)S(1)}, bf16[96,2,256]{2,1,0:T(2,128)(2,1)S(1)}, u32[]{:S(2)}, u32[]{:S(2)}) collective-permute-start(bf16[96,2,256]{2,1,0:T(2,128)(2,1)S(1)} %get-tuple-element.7), channel_id=1, source_target_pairs={{0,4},{4,8},{8,12},{12,0},{1,5},{5,9},{9,13},{13,1},{2,6},{6,10},{... | collective-permute-start | bytes 294920 | tf_op jit(solution)/shard_map/ppermute | solution.py:27
  113.8 6.4 %collective-permute-start.1 = (bf16[96,2,256]{2,1,0:T(2,128)(2,1)S(1)}, bf16[96,2,256]{2,1,0:T(2,128)(2,1)S(1)}, u32[]{:S(2)}, u32[]{:S(2)}) collective-permute-start(bf16[96,2,256]{2,1,0:T(2,128)(2,1)S(1)} %get-tuple-element.8), channel_id=1, source_target_pairs={{4,0},{8,4},{12,8},{0,12},{5,1},{9,5},{13,9},{1,13},{6,2},{10,6},{... | collective-permute-start | bytes 294920 | tf_op jit(solution)/shard_map/ppermute | solution.py:28
  121.0 5.9 %collective-permute-start.2 = (bf16[2,32,256]{2,1,0:T(8,128)(2,1)S(1)}, bf16[2,32,256]{2,1,0:T(8,128)(2,1)S(1)}, u32[]{:S(2)}, u32[]{:S(2)}) collective-permute-start(bf16[2,32,256]{2,1,0:T(8,128)(2,1)S(1)} %get-tuple-element.5), channel_id=1, source_target_pairs={{0,1},{1,2},{2,3},{4,5},{5,6},{6,7},{8,9},{9,10},{10,11},{12,13},{... | collective-permute-start | bytes 98312 | tf_op jit(solution)/shard_map/ppermute | solution.py:27
  124.8 6.6 %copy-start = (bf16[256,2048]{1,0:T(8,128)(2,1)S(1)}, bf16[256,2048]{1,0:T(8,128)(2,1)}, u32[]{:S(2)}) copy-start(bf16[256,2048]{1,0:T(8,128)(2,1)} %w_in.1) | copy-start | bytes 3145732
  124.8 6.6 %copy-start.1 = (bf16[1024,256]{1,0:T(8,128)(2,1)S(1)}, bf16[1024,256]{1,0:T(8,128)(2,1)}, u32[]{:S(2)}) copy-start(bf16[1024,256]{1,0:T(8,128)(2,1)} %w_down.1) | copy-start | bytes 1572868
  124.8 6.6 %copy-start.2 = (f32[25,256]{1,0:T(8,128)S(1)}, f32[25,256]{1,0:T(8,128)}, u32[]{:S(2)}) copy-start(f32[25,256]{1,0:T(8,128)} %taps.1) | copy-start | bytes 76804
  124.8 6.6 %copy-start.3 = (f32[3,256]{1,0:T(4,128)S(1)}, f32[3,256]{1,0:T(4,128)}, u32[]{:S(2)}) copy-start(f32[3,256]{1,0:T(4,128)} %gains.3) | copy-start | bytes 9220
  124.8 5.4 %collective-permute-start.3 = (bf16[2,32,256]{2,1,0:T(8,128)(2,1)S(1)}, bf16[2,32,256]{2,1,0:T(8,128)(2,1)S(1)}, u32[]{:S(2)}, u32[]{:S(2)}) collective-permute-start(bf16[2,32,256]{2,1,0:T(8,128)(2,1)S(1)} %get-tuple-element.6), channel_id=1, source_target_pairs={{1,0},{2,1},{3,2},{5,4},{6,5},{7,6},{9,8},{10,9},{11,10},{13,12},{... | collective-permute-start | bytes 98312 | tf_op jit(solution)/shard_map/ppermute | solution.py:28

commit v3 on v2

--- a/solution.py
+++ b/solution.py
@@ -15,19 +15,6 @@
 F32, BF16 = jnp.float32, jnp.bfloat16
 NT = (((1,), (1,)), ((), ()))
 TN = (((0,), (0,)), ((), ()))
-
-
-def extended(x, sides, width, wrap):
-    for axis, dim in sides:
-        count, length = (lax.axis_size(axis), x.shape[dim])
-        up = [(i, (i + 1) % count) for i in range(count if wrap else count - 1)]
-        down = [(j, i) for i, j in up]
-        last = lax.slice_in_dim(x, length - width, length, axis=dim)
-        leading = lax.slice_in_dim(x, 0, width, axis=dim)
-        before = lax.ppermute(last, axis, up)
-        after = lax.ppermute(leading, axis, down)
-        x = jnp.concatenate([before, x, after], axis=dim)
-    return x
 
 
 def layer_norm(values, gains):
@@ -65,8 +52,8 @@
     n, m, heads, lon_cols, chunk,
     x_ref, gains, wqkv1, wo1, wqkv2, wo2, scales,
     out_ref,
-    xs, recv, wide, mixed, obuf, ret, state, lsend, lrecv, lout, lret, wvt1, wvt2,
-    fs, fr, bs, br, gs, gr, hs, hr,
+    xs, recv, wide, mixed, obuf, ret, state, lsend, lrecv, lout, lret, wvt1, wvt2, esend, erecv, hrecv,
+    fs, fr, bs, br, gs, gr, hs, hr, es, er, rs, rr,
 ):
     rows_own = xs.shape[1]
     width, features = xs.shape[2], xs.shape[3]
@@ -121,12 +108,44 @@
             device_id={"lat": peer}, device_id_type=MESH,
         )
 
+    margin = KERNEL // 2
+    left, right = lax.rem(me + n - 1, n), lax.rem(me + 1, n)
+    above, below = lax.rem(mine + m - 1, m), lax.rem(mine + 1, m)
+
+    def edge(side):
+        return pltpu.make_async_remote_copy(
+            src_ref=esend.at[side], dst_ref=erecv.at[1 - side],
+            send_sem=es.at[side], recv_sem=er.at[1 - side],
+            device_id={"lon": (left, right)[side]}, device_id_type=MESH,
+        )
+
+    def border(side):
+        start = (margin, lat_rows)[side]
+        return pltpu.make_async_remote_copy(
+            src_ref=out_ref.at[pl.ds(start, margin)], dst_ref=hrecv.at[1 - side],
+            send_sem=rs.at[side], recv_sem=rr.at[1 - side],
+            device_id={"lat": (above, below)[side]}, device_id_type=MESH,
+        )
+
+    def rows_of(first, count):
+        block = x_ref[pl.ds(first, count)].astype(F32)
+        spare_cols = jnp.zeros((count, width - lon_cols, features), F32)
+        return jnp.concatenate([block, spare_cols], 1)
+
+    def send_edges():
+        for side, base in enumerate((margin, lon_cols)):
+            for k in range(margin):
+                for half in range(halves):
+                    column = wide.at[half][pl.ds(base + k, lat_rows, stride=width), :]
+                    esend[side, k, :, half * LANES : (half + 1) * LANES] = column.astype(BF16)
+            edge(side).start()
+
     @pl.loop(0, chunks)
     def _(ch):
         part = pl.ds(ch * chunk, chunk)
         for o in range(n):
             first_row = o * rows_own + ch * chunk
-            block = x_ref[pl.ds(first_row, chunk)].astype(F32)
+            block = rows_of(first_row, chunk)
             xs[o, part] = layer_norm(block, gains[0:1][None]).astype(BF16)
         for d in range(n - 1):
             forth(ch, d).start()
@@ -137,7 +156,7 @@
 
     @pl.loop(0, lat_rows // chunk)
     def _(i):
-        block = x_ref[pl.ds(i * chunk, chunk)].astype(F32).reshape(chunk * width, features)
+        block = rows_of(i * chunk, chunk).reshape(chunk * width, features)
         place = pl.ds(pl.multiple_of(i * (chunk * width), chunk * width), chunk * width)
         for half in range(halves):
             wide[half, place, :] = block[:, half * LANES : (half + 1) * LANES]
@@ -170,8 +189,12 @@
 
     spare = segment - m * rows_own
 
+    def group(t):
+        return lax.rem(t + (cols_own - margin), cols_own)
+
     @pl.loop(0, cols_own)
-    def _(c):
+    def _(t):
+        c = group(t)
         for j in range(n):
             for half in range(halves):
                 pieces = []
@@ -220,32 +243,82 @@
             lat_back(c, d).wait_recv()
         for p in range(m):
             total = (state[c, p] + lret[p, c].astype(F32)).astype(BF16).astype(F32)
-            place = pl.ds(p * cols_own + c, lat_rows, stride=width)
+            place = pl.ds(margin + p * cols_own + c, lat_rows, stride=width)
             for half in range(halves):
                 wide.at[half][place, :] = total[:, half * LANES : (half + 1) * LANES]
 
-    finish_lon(0)
+    finish_lon(group(0))
 
     @pl.loop(0, cols_own)
-    def _(c):
-        @pl.when(c < cols_own - 1)
-        def _():
-            finish_lon(c + 1)
-
-        lat_line(c)
-
-        @pl.when(c > 0)
-        def _():
-            finish_lat(c - 1)
-
-    finish_lat(cols_own - 1)
-
-    @pl.loop(0, lat_rows // chunk)
+    def _(t):
+        @pl.when(t < cols_own - 1)
+        def _():
+            finish_lon(group(t + 1))
+
+        lat_line(group(t))
+
+        @pl.when(t > 0)
+        def _():
+            finish_lat(group(t - 1))
+
+        if cols_own > 2 * margin:
+
+            @pl.when(t == 2 * margin)
+            def _():
+                send_edges()
+
+    finish_lat(group(cols_own - 1))
+    if cols_own <= 2 * margin:
+        send_edges()
+
+    for side, base in enumerate((0, margin + lon_cols)):
+        edge(1 - side).wait_recv()
+        for k in range(margin):
+            for half in range(halves):
+                column = erecv[side, k, :, half * LANES : (half + 1) * LANES].astype(F32)
+                wide.at[half][pl.ds(base + k, lat_rows, stride=width), :] = column
+
+    def emit(first, count):
+        place = pl.ds(first * width, count * width)
+        for half in range(halves):
+            block = wide[half, place, :].astype(BF16).reshape(count, width, LANES)
+            out_ref[pl.ds(margin + first, count), :, half * LANES : (half + 1) * LANES] = block
+
+    ends = (mine > 0, mine < m - 1)
+    for side, first in enumerate((0, lat_rows - margin)):
+        emit(first, margin)
+
+        @pl.when(ends[side])
+        def _():
+            border(side).start()
+
+    count = next(size for size in (4, 2, 1) if (lat_rows - 2 * margin) % size == 0)
+
+    @pl.loop(0, (lat_rows - 2 * margin) // count)
     def _(i):
-        place = pl.ds(pl.multiple_of(i * (chunk * width), chunk * width), chunk * width)
+        first = margin + i * count
+        place = pl.ds(pl.multiple_of(first * width, width), count * width)
         for half in range(halves):
-            block = wide[half, place, :].astype(BF16).reshape(chunk, width, LANES)
-            out_ref[pl.ds(i * chunk, chunk), :, half * LANES : (half + 1) * LANES] = block
+            block = wide[half, place, :].astype(BF16).reshape(count, width, LANES)
+            out_ref[pl.ds(margin + first, count), :, half * LANES : (half + 1) * LANES] = block
+
+    for side, first in enumerate((0, margin + lat_rows)):
+
+        @pl.when(ends[side])
+        def _():
+            border(1 - side).wait_recv()
+            out_ref[pl.ds(first, margin)] = hrecv[side]
+
+        @pl.when(jnp.logical_not(ends[side]))
+        def _():
+            out_ref[pl.ds(first, margin)] = jnp.zeros((margin, width, features), BF16)
+
+    for side in range(2):
+        edge(side).wait_send()
+
+        @pl.when(ends[side])
+        def _():
+            border(side).wait_send()
 
     @pl.loop(0, chunks)
     def _(ch):
@@ -265,17 +338,17 @@
     lat_rows, lon_cols, features = fields.shape
     heads = logit_scales.shape[1]
     n, m = lax.axis_size("lon"), lax.axis_size("lat")
-    width = -(-lon_cols // 16) * 16
+    margin = KERNEL // 2
+    width = -(-(lon_cols + 2 * margin) // 16) * 16
     rows_own, cols_own = lat_rows // n, lon_cols // m
     chunk = next(size for size in (4, 3, 2, 1) if rows_own % size == 0)
     chunks, halves = rows_own // chunk, features // LANES
     segment = -(-(m * rows_own) // 16) * 16
-    padded = jnp.pad(fields, ((0, 0), (0, width - lon_cols), (0, 0)))
     vmem = pl.BlockSpec(memory_space=pltpu.VMEM)
     dma = pltpu.SemaphoreType.DMA
     return pl.pallas_call(
         functools.partial(attention_kernel, n, m, heads, lon_cols, chunk),
-        out_shape=jax.ShapeDtypeStruct((lat_rows, width, features), BF16),
+        out_shape=jax.ShapeDtypeStruct((lat_rows + 2 * margin, width, features), BF16),
         in_specs=[vmem] * 6 + [pl.BlockSpec(memory_space=pltpu.SMEM)],
         out_specs=vmem,
         scratch_shapes=[
@@ -292,15 +365,19 @@
             pltpu.VMEM((m, cols_own, lat_rows, features), BF16),
             pltpu.VMEM((features, features), BF16),
             pltpu.VMEM((features, features), BF16),
+            pltpu.VMEM((2, margin, lat_rows, features), BF16),
+            pltpu.VMEM((2, margin, lat_rows, features), BF16),
+            pltpu.VMEM((2, margin, width, features), BF16),
             dma((chunks, n - 1)), dma((chunks, n - 1)),
             dma((cols_own, n - 1)), dma((cols_own, n - 1)),
             dma((cols_own, m - 1)), dma((cols_own, m - 1)),
             dma((cols_own, m - 1)), dma((cols_own, m - 1)),
+            dma((2,)), dma((2,)), dma((2,)), dma((2,)),
         ],
         compiler_params=pltpu.CompilerParams(
             collective_id=0, has_side_effects=True, vmem_limit_bytes=60 * 2**20
         ),
-    )(padded, norm_gains, lon_qkv, lon_out, lat_qkv, lat_out, logit_scales)
+    )(fields, norm_gains, lon_qkv, lon_out, lat_qkv, lat_out, logit_scales)
 
 
 def mixer_kernel(rows, lon_cols, wide, taps, gains, w_in, w_down, out):
@@ -329,13 +406,9 @@
     out[...] = total[:, :lon_cols].astype(BF16)
 
 
-def mixer(second, conv_taps, norm_gains, mlp_in, mlp_down):
-    lat_rows, lon_cols, features = second.shape
-    margin = KERNEL // 2
-    widened = extended(second, (("lon", 1),), margin, True)
-    widened = extended(widened, (("lat", 0),), margin, False)
-    width = -(-widened.shape[1] // 16) * 16
-    widened = jnp.pad(widened, ((0, 0), (0, width - widened.shape[1]), (0, 0)))
+def mixer(widened, lon_cols, conv_taps, norm_gains, mlp_in, mlp_down):
+    features = widened.shape[2]
+    lat_rows = widened.shape[0] - KERNEL + 1
     rows = next(r for r in (8, 6, 4, 3, 2, 1) if lat_rows % r == 0)
     vmem = pl.BlockSpec(memory_space=pltpu.VMEM)
     return pl.pallas_call(
@@ -344,7 +417,7 @@
         out_shape=jax.ShapeDtypeStruct((lat_rows, lon_cols, features), BF16),
         in_specs=[vmem] * 5,
         out_specs=pl.BlockSpec((rows, lon_cols, features), lambda i: (i, 0, 0)),
-        compiler_params=pltpu.CompilerParams(vmem_limit_bytes=48 * 2**20),
+        compiler_params=pltpu.CompilerParams(vmem_limit_bytes=60 * 2**20),
     )(widened, conv_taps, norm_gains, mlp_in, mlp_down)
 
 
@@ -352,8 +425,8 @@
     fields, norm_gains, lon_qkv, lon_out, lat_qkv, lat_out, logit_scales, conv_taps, mlp_in, mlp_down
 ):
     lon_cols = fields.shape[1]
-    second = attention(fields, norm_gains, lon_qkv, lon_out, lat_qkv, lat_out, logit_scales)
-    return mixer(second[:, :lon_cols], conv_taps, norm_gains, mlp_in, mlp_down)
+    widened = attention(fields, norm_gains, lon_qkv, lon_out, lat_qkv, lat_out, logit_scales)
+    return mixer(widened, lon_cols, conv_taps, norm_gains, mlp_in, mlp_down)
 
 
 def solution(mesh):

time: 151 us -> 138 us (0.914)
  waiting for transfers between devices: 8.24 us -> 0 us
  starting transfers between devices: 7.34 us -> 0 us
  Pallas kernels: 126 us -> 131 us
  other arithmetic: 1.96 us -> 0 us
    ppermute x4 -> x0, waiting for transfers between devices: 8.24 us -> none  [the longest x2 5.16 us: extended(): after = lax.ppermute(leading, axis, down)]
    ppermute x4 -> x0, starting transfers between devices: 7.34 us -> none  [the longest x2 3.82 us: extended(): before = lax.ppermute(last, axis, up)]
    pallas_call x1, Pallas kernels: 17.1 us -> 19.8 us  [mixer(): pl.pallas_call(functools.partial(mixer_kernel, rows, lon_cols), grid=(lat...]
    pallas_call x1, Pallas kernels: 109 us -> 111 us  [attention(): pl.pallas_call(functools.partial(attention_kernel, n, m, heads, lon_cols,...]
    unnamed x11 -> x1, local copies, waits for them, and re-layouts: 2.14 us -> 3.27 us
  transfers between devices with their start and end apart: 4 -> 0, of which waited for: 3 -> 0; matrix products, arithmetic and copies ran while one was open for 0% -> 0% of each run, Pallas kernels for 0% -> 0%
where the time goes in v3:
time: 138 us
  Pallas kernels  131 us (95%)
  local copies, waits for them, and re-layouts  6.52 us (5%)
    pallas_call x1, Pallas kernels, attention(): pl.pallas_call(functools.partial(attention_kernel, n, m, heads, lon_cols,...  111 us
    pallas_call x1, Pallas kernels, mixer(): pl.pallas_call(functools.partial(mixer_kernel, rows, lon_cols), grid=(lat...  19.8 us
    unnamed x1, local copies, waits for them, and re-layouts  3.27 us
    pallas_call x1, local copies, waits for them, and re-layouts, mixer(): pl.pallas_call(functools.partial(mixer_kernel, rows, lon_cols), grid=(lat...  3.25 us

profile of v3, /device:TPU:25, one launch (start us, length us, event | category | flops | bytes accessed | tf_op | source)
XLA Modules:
  0.0 137.7 jit_solution(9473134082933056175)
XLA Ops:
  0.0 3.3 %copy.11.x_ref = bf16[96,28,256]{2,1,0:T(8,128)(2,1)} copy(bf16[96,28,256]{2,0,1:T(8,128)(2,1)} %param.10) | data formatting | bytes 2752512 | tf_op args[0]
  3.3 111.4 %shard_map.100.wide = bf16[100,32,256]{2,1,0:T(8,128)(2,1)} custom-call(bf16[96,28,256]{2,1,0:T(8,128)(2,1)} %copy.11.x_ref, f32[3,256]{1,0:T(4,128)} %gains.3, bf16[256,768]{1,0:T(8,128)(2,1)} %wqkv1.1, bf16[256,256]{1,0:T(8,128)(2,1)} %wo1.1, bf16[256,768]{1,0:T(8,128)(2,1)} %wqkv2.1, bf16[256,256]{1,0:T(8,128)(2,1)} %wo2.1, f32[2,8]{1,0:T(2,128)} %scales.1), custom_call_target="tpu_custom_call" | custom-call | tf_op jit(solution)/shard_map/pallas_call | solution.py:349
  114.7 19.8 %shard_map.101 = bf16[96,28,256]{2,1,0:T(8,128)(2,1)} custom-call(bf16[100,32,256]{2,1,0:T(8,128)(2,1)} %shard_map.100.wide, f32[25,256]{1,0:T(8,128)} %taps.1, f32[3,256]{1,0:T(4,128)} %gains.3, bf16[256,2048]{1,0:T(8,128)(2,1)} %w_in.1, bf16[1024,256]{1,0:T(8,128)(2,1)} %w_down.1), custom_call_target="tpu_custom_call" | custom-call | tf_op jit(solution)/shard_map/pallas_call | solution.py:414
  134.4 3.2 %copy.12 = bf16[96,28,256]{2,0,1:T(8,128)(2,1)} copy(bf16[96,28,256]{2,1,0:T(8,128)(2,1)} %shard_map.101) | data formatting | bytes 2752512 | tf_op jit(solution)/shard_map/pallas_call | solution.py:414

commit v4 on v3

v4 whole, which is shorter than its diff:
```python
import functools
import math

import jax
import jax.numpy as jnp
from jax import lax
from jax.experimental import pallas as pl
from jax.experimental.pallas import tpu as pltpu
from jax.sharding import PartitionSpec as P

KERNEL = 5
LANES = 128
EPSILON = 1e-05
MESH = pl.DeviceIdType.MESH
F32, BF16 = jnp.float32, jnp.bfloat16
NT = (((1,), (1,)), ((), ()))
TN = (((0,), (0,)), ((), ()))


def layer_norm(values, gains):
    average = jnp.mean(values, -1, keepdims=True)
    centred = values - average
    spread = jnp.mean(centred * centred, -1, keepdims=True)
    return centred * lax.rsqrt(spread + EPSILON) * gains


def attend(x, wqk, wvt, wout, factor_of, heads):
    features = x.shape[-1]
    size = features // heads
    qk = jnp.dot(x, wqk, preferred_element_type=F32).astype(BF16)
    queries, keys = qk[:, :features], qk[:, features:]
    values = lax.dot_general(wvt, x, NT, preferred_element_type=F32).astype(BF16)
    lane = lax.broadcasted_iota(jnp.int32, (1, features), 1) // size
    parts = []
    for h in range(heads):
        own = keys * (lane == h).astype(F32).astype(BF16)
        scores = lax.dot_general(own, queries, NT, preferred_element_type=F32)
        top = jnp.max(scores, 0, keepdims=True)
        weights = jnp.exp2((scores - top) * (factor_of(h) * math.log2(math.e)))
        total = jnp.sum(weights, 0, keepdims=True)
        part = jnp.dot(
            values[h * size : (h + 1) * size], weights.astype(BF16), preferred_element_type=F32
        )
        parts.append(part / total)
    context = jnp.concatenate(parts, 0).astype(BF16)
    return lax.dot_general(context, wout, TN, preferred_element_type=F32)


def attention_kernel(
    n, m, heads, lon_cols, chunk,
    x_ref, gains, wqkv1, wo1, wqkv2, wo2, scales,
    out_ref, halo_ref,
    xs, recv, normed, stage, lines, mixed, obuf, ret, state, lsend, lrecv, lout, lret, wvt1, wvt2, erecv, rims, hsend, hrecv,
    fs, fr, bs, br, gs, gr, hs, hr, es, er, rs, rr,
):
    lat_rows, features = x_ref.shape[1:]
    rows_own = lat_rows // n
    chunks = rows_own // chunk
    tokens = xs.shape[2]
    slot = tokens // lon_cols
    width = lon_cols + KERNEL - 1
    cols_own = lon_cols // m
    halves = features // LANES
    split = 2 * features
    segment = obuf.shape[2]
    me = lax.axis_index("lon")
    mine = lax.axis_index("lat")
    lon_peers = [lax.rem(me + d, n) for d in range(1, n)]
    lat_peers = [lax.rem(mine + d, m) for d in range(1, m)]

    barrier = pltpu.get_barrier_semaphore()
    for peer in lon_peers:
        pl.semaphore_signal(barrier, inc=1, device_id={"lon": peer}, device_id_type=MESH)
    for peer in lat_peers:
        pl.semaphore_signal(barrier, inc=1, device_id={"lat": peer}, device_id_type=MESH)
    pl.semaphore_wait(barrier, n + m - 2)

    def forth(ch, d):
        peer = lon_peers[d]
        return pltpu.make_async_remote_copy(
            src_ref=xs.at[peer, ch], dst_ref=recv.at[me, ch],
            send_sem=fs.at[ch, d], recv_sem=fr.at[ch, d],
            device_id={"lon": peer}, device_id_type=MESH,
        )

    def back(c, d):
        peer = lon_peers[d]
        return pltpu.make_async_remote_copy(
            src_ref=obuf.at[peer, c], dst_ref=ret.at[me, c],
            send_sem=bs.at[c, d], recv_sem=br.at[c, d],
            device_id={"lon": peer}, device_id_type=MESH,
        )

    def lat_forth(c, d):
        peer = lat_peers[d]
        return pltpu.make_async_remote_copy(
            src_ref=lsend.at[peer, c], dst_ref=lrecv.at[mine, c],
            send_sem=gs.at[c, d], recv_sem=gr.at[c, d],
            device_id={"lat": peer}, device_id_type=MESH,
        )

    def lat_back(c, d):
        peer = lat_peers[d]
        return pltpu.make_async_remote_copy(
            src_ref=lout.at[peer, c], dst_ref=lret.at[mine, c],
            send_sem=hs.at[c, d], recv_sem=hr.at[c, d],
            device_id={"lat": peer}, device_id_type=MESH,
        )

    margin = KERNEL // 2
    left, right = lax.rem(me + n - 1, n), lax.rem(me + 1, n)
    above, below = lax.rem(mine + m - 1, m), lax.rem(mine + 1, m)

    def edge(side):
        start = (margin, lon_cols)[side]
        return pltpu.make_async_remote_copy(
            src_ref=out_ref.at[pl.ds(start, margin)], dst_ref=erecv.at[1 - side],
            send_sem=es.at[side], recv_sem=er.at[1 - side],
            device_id={"lon": (left, right)[side]}, device_id_type=MESH,
        )

    def border(side):
        return pltpu.make_async_remote_copy(
            src_ref=hsend.at[side], dst_ref=hrecv.at[1 - side],
            send_sem=rs.at[side], recv_sem=rr.at[1 - side],
            device_id={"lat": (above, below)[side]}, device_id_type=MESH,
        )

    def lanes(half):
        return slice(half * LANES, (half + 1) * LANES)

    @pl.loop(0, lon_cols)
    def _(col):
        block = layer_norm(x_ref[col].astype(F32), gains[0:1])
        place = pl.ds(pl.multiple_of(col * lat_rows, 8), lat_rows)
        for half in range(halves):
            normed[half, place, :] = block[:, lanes(half)]

    if slot > chunk:
        stage[...] = jnp.zeros(stage.shape, F32)

    @pl.loop(0, chunks)
    def _(ch):
        for o in range(n):
            for half in range(halves):
                for i in range(chunk):
                    row = o * rows_own + ch * chunk + i
                    taken = normed.at[half][pl.ds(row, lon_cols, stride=lat_rows), :]
                    stage.at[o % 2, half][pl.ds(i, lon_cols, stride=slot), :] = taken
                xs[o, ch, :, lanes(half)] = stage[o % 2, half].astype(BF16)
        for d in range(n - 1):
            forth(ch, d).start()
        recv[me, ch] = xs[me, ch]

    wvt1[...] = wqkv1[:, split:].astype(F32).T.astype(BF16)
    wvt2[...] = wqkv2[:, split:].astype(F32).T.astype(BF16)

    @pl.loop(0, chunks)
    def _(ch):
        for d in range(n - 1):
            forth(ch, d).wait_recv()
        for j in range(n):
            for half in range(halves):
                arrived = recv[j, ch, :, lanes(half)].astype(F32)
                lines[half, j * tokens : (j + 1) * tokens, :] = arrived

        @pl.loop(0, chunk)
        def _(i):
            place = pl.ds(i, n * lon_cols, stride=slot)
            line = jnp.concatenate(
                [lines.at[half][place, :] for half in range(halves)], 1
            ).astype(BF16)
            result = attend(
                line, wqkv1[:, :split], wvt1[...], wo1[...], lambda h: scales[0, h], heads
            )
            place = pl.ds(ch * chunk + i, n * lon_cols, stride=rows_own)
            for half in range(halves):
                mixed.at[half][place, :] = result[:, lanes(half)]

    spare = segment - m * rows_own

    def group(t):
        return lax.rem(t + (cols_own - margin), cols_own)

    @pl.loop(0, cols_own)
    def _(t):
        c = group(t)
        for j in range(n):
            for half in range(halves):
                pieces = []
                for p in range(m):
                    start = (j * lon_cols + p * cols_own + c) * rows_own
                    if rows_own % 8 == 0:
                        start = pl.multiple_of(start, 8)
                    pieces.append(mixed[half, pl.ds(start, rows_own), :])
                if spare:
                    pieces.append(jnp.zeros((spare, LANES), F32))
                block = jnp.concatenate(pieces, 0).astype(BF16)
                obuf[j, c, :, lanes(half)] = block
        for d in range(n - 1):
            back(c, d).start()
        ret[me, c] = obuf[me, c]

    def finish_lon(c):
        for d in range(n - 1):
            back(c, d).wait_recv()
        arrived = [ret[o, c].astype(F32) for o in range(n)]
        for p in range(m):
            lon_mix = jnp.concatenate(
                [block[p * rows_own : (p + 1) * rows_own] for block in arrived], 0
            )
            first = (x_ref[p * cols_own + c].astype(F32) + lon_mix).astype(BF16).astype(F32)
            state[c, p] = first
            lsend[p, c] = layer_norm(first, gains[1:2]).astype(BF16)
        for d in range(m - 1):
            lat_forth(c, d).start()
        lrecv[mine, c] = lsend[mine, c]

    def lat_line(c):
        for d in range(m - 1):
            lat_forth(c, d).wait_recv()
        line = lrecv[:, c].reshape(m * lat_rows, features)
        result = attend(
            line, wqkv2[:, :split], wvt2[...], wo2[...], lambda h: scales[1, h], heads
        )
        lout[:, c] = result.astype(BF16).reshape(m, lat_rows, features)
        for d in range(m - 1):
            lat_back(c, d).start()
        lret[mine, c] = lout[mine, c]

    def keep_rims(col, block):
        place = pl.ds(pl.multiple_of(col * 8, 8), 8)
        for half in range(halves):
            rims[0, half, place, :] = block[:8, lanes(half)]
            rims[1, half, place, :] = block[lat_rows - 8 :, lanes(half)]

    def finish_lat(c):
        for d in range(m - 1):
            lat_back(c, d).wait_recv()
        for p in range(m):
            total = (state[c, p] + lret[p, c].astype(F32)).astype(BF16)
            col = margin + p * cols_own + c
            out_ref[col] = total
            keep_rims(col, total.astype(F32))

    finish_lon(group(0))

    @pl.loop(0, cols_own)
    def _(t):
        @pl.when(t < cols_own - 1)
        def _():
            finish_lon(group(t + 1))

        lat_line(group(t))

        @pl.when(t > 0)
        def _():
            finish_lat(group(t - 1))

        if cols_own > 2 * margin:

            @pl.when(t == 2 * margin)
            def _():
                for side in range(2):
                    edge(side).start()

    finish_lat(group(cols_own - 1))
    if cols_own <= 2 * margin:
        for side in range(2):
            edge(side).start()

    for side, base in enumerate((0, margin + lon_cols)):
        edge(1 - side).wait_recv()
        for k in range(margin):
            out_ref[base + k] = erecv[side, k]
            keep_rims(base + k, erecv[side, k].astype(F32))

    ends = (mine > 0, mine < m - 1)
    for side, base in enumerate((0, 8 - margin)):
        for k in range(margin):
            for half in range(halves):
                row = rims.at[side, half][pl.ds(base + k, width, stride=8), :]
                hsend[side, k, :, lanes(half)] = row.astype(BF16)

        @pl.when(ends[side])
        def _():
            border(side).start()

    halo_ref[...] = jnp.zeros(halo_ref.shape, F32)
    for side, base in enumerate((8 - margin, 0)):

        @pl.when(ends[side])
        def _():
            border(1 - side).wait_recv()
            for k in range(margin):
                for half in range(halves):
                    row = hrecv[side, k, :, lanes(half)].astype(F32)
                    halo_ref.at[side, half][pl.ds(base + k, width, stride=8), :] = row

    for side in range(2):
        edge(side).wait_send()

        @pl.when(ends[side])
        def _():
            border(side).wait_send()

    @pl.loop(0, chunks)
    def _(ch):
        for d in range(n - 1):
            forth(ch, d).wait_send()

    @pl.loop(0, cols_own)
    def _(c):
        for d in range(n - 1):
            back(c, d).wait_send()
        for d in range(m - 1):
            lat_forth(c, d).wait_send()
            lat_back(c, d).wait_send()


def attention(fields, norm_gains, lon_qkv, lon_out, lat_qkv, lat_out, logit_scales):
    lon_cols, lat_rows, features = fields.shape
    heads = logit_scales.shape[1]
    n, m = lax.axis_size("lon"), lax.axis_size("lat")
    margin = KERNEL // 2
    width = lon_cols + 2 * margin
    rows_own, cols_own = lat_rows // n, lon_cols // m
    chunk = next(size for size in (4, 3, 2, 1) if rows_own % size == 0)
    slot = chunk
    while lon_cols * slot % 16:
        slot += 1
    tokens = lon_cols * slot
    chunks, halves = rows_own // chunk, features // LANES
    segment = -(-(m * rows_own) // 16) * 16
    vmem = pl.BlockSpec(memory_space=pltpu.VMEM)
    dma = pltpu.SemaphoreType.DMA
    groups = (m, cols_own, lat_rows, features)
    return pl.pallas_call(
        functools.partial(attention_kernel, n, m, heads, lon_cols, chunk),
        out_shape=(
            jax.ShapeDtypeStruct((width, lat_rows, features), BF16),
            jax.ShapeDtypeStruct((2, halves, width * 8, LANES), F32),
        ),
        in_specs=[vmem] * 6 + [pl.BlockSpec(memory_space=pltpu.SMEM)],
        out_specs=(vmem, vmem),
        scratch_shapes=[
            pltpu.VMEM((n, chunks, tokens, features), BF16),
            pltpu.VMEM((n, chunks, tokens, features), BF16),
            pltpu.VMEM((halves, lon_cols * lat_rows, LANES), F32),
            pltpu.VMEM((2, halves, tokens, LANES), F32),
            pltpu.VMEM((halves, n * tokens, LANES), F32),
            pltpu.VMEM((halves, n * lon_cols * rows_own, LANES), F32),
            pltpu.VMEM((n, cols_own, segment, features), BF16),
            pltpu.VMEM((n, cols_own, segment, features), BF16),
            pltpu.VMEM((cols_own, m, lat_rows, features), F32),
            pltpu.VMEM(groups, BF16),
            pltpu.VMEM(groups, BF16),
            pltpu.VMEM(groups, BF16),
            pltpu.VMEM(groups, BF16),
            pltpu.VMEM((features, features), BF16),
            pltpu.VMEM((features, features), BF16),
            pltpu.VMEM((2, margin, lat_rows, features), BF16),
            pltpu.VMEM((2, halves, width * 8, LANES), F32),
            pltpu.VMEM((2, margin, width, features), BF16),
            pltpu.VMEM((2, margin, width, features), BF16),
            dma((chunks, n - 1)), dma((chunks, n - 1)),
            dma((cols_own, n - 1)), dma((cols_own, n - 1)),
            dma((cols_own, m - 1)), dma((cols_own, m - 1)),
            dma((cols_own, m - 1)), dma((cols_own, m - 1)),
            dma((2,)), dma((2,)), dma((2,)), dma((2,)),
        ],
        compiler_params=pltpu.CompilerParams(
            collective_id=0, has_side_effects=True, vmem_limit_bytes=60 * 2**20
        ),
    )(fields, norm_gains, lon_qkv, lon_out, lat_qkv, lat_out, logit_scales)


def mixer_kernel(cols, wide, halo, taps, gains, w_in, w_down, out):
    first = pl.program_id(0) * cols
    rows, features = wide.shape[1:]
    hidden_len = w_down.shape[0]
    margin = KERNEL // 2
    count = cols + 2 * margin
    body = wide[pl.ds(first, count)].astype(F32)
    place = pl.ds(pl.multiple_of(first * 8, 8), count * 8)
    rims = [
        jnp.concatenate([halo[side, half, place, :] for half in range(features // LANES)], 1)
        for side in range(2)
    ]
    rims = [rim.reshape(count, 8, features) for rim in rims]
    lines = jnp.concatenate([rims[0], body, rims[1]], 1)
    smoothed = None
    for dy in range(KERNEL):
        term = None
        for dx in range(KERNEL):
            tap = taps[pl.ds(dy * KERNEL + dx, 1), :][None]
            piece = tap * lines[dx : dx + cols]
            term = piece if term is None else term + piece
        term = term[:, 8 - margin + dy : 8 - margin + dy + rows]
        smoothed = term if smoothed is None else smoothed + term
    normed = layer_norm(smoothed.reshape(cols * rows, features), gains[2:3]).astype(BF16)
    gate_up = jnp.dot(normed, w_in[...], preferred_element_type=F32)
    half = gate_up[:, :hidden_len] * 0.5
    hidden = (half * (1.0 + jnp.tanh(half)) * gate_up[:, hidden_len:]).astype(BF16)
    update = jnp.dot(hidden, w_down[...], preferred_element_type=F32)
    total = body[margin : margin + cols] + update.reshape(cols, rows, features)
    out[...] = total.astype(BF16)


def mixer(widened, halo, conv_taps, norm_gains, mlp_in, mlp_down):
    width, lat_rows, features = widened.shape
    lon_cols = width - KERNEL + 1
    cols = next(size for size in (4, 3, 2, 1) if lon_cols % size == 0)
    vmem = pl.BlockSpec(memory_space=pltpu.VMEM)
    return pl.pallas_call(
        functools.partial(mixer_kernel, cols),
        grid=(lon_cols // cols,),
        out_shape=jax.ShapeDtypeStruct((lon_cols, lat_rows, features), BF16),
        in_specs=[vmem] * 6,
        out_specs=pl.BlockSpec((cols, lat_rows, features), lambda i: (i, 0, 0)),
        compiler_params=pltpu.CompilerParams(vmem_limit_bytes=60 * 2**20),
    )(widened, halo, conv_taps, norm_gains, mlp_in, mlp_down)


def per_device(
    fields, norm_gains, lon_qkv, lon_out, lat_qkv, lat_out, logit_scales, conv_taps, mlp_in, mlp_down
):
    columns = jnp.swapaxes(fields, 0, 1)
    widened, halo = attention(
        columns, norm_gains, lon_qkv, lon_out, lat_qkv, lat_out, logit_scales
    )
    return jnp.swapaxes(mixer(widened, halo, conv_taps, norm_gains, mlp_in, mlp_down), 0, 1)


def solution(mesh):
    in_specs = (P(("groups", "lat"), "lon", None), P(), P(), P(), P(), P(), P(), P(), P(), P())
    out_specs = P(("groups", "lat"), "lon", None)
    return jax.shard_map(
        per_device, mesh=mesh, in_specs=in_specs, out_specs=out_specs, check_vma=False
    )
```

time: 138 us -> 135 us (0.978)
  local copies, waits for them, and re-layouts: 6.52 us -> 0 us
  Pallas kernels: 131 us -> 134 us
    pallas_call x1, Pallas kernels: 111 us -> 117 us  [attention(): pl.pallas_call(functools.partial(attention_kernel, n, m, heads, lon_cols,...]
    unnamed x1 -> x0, local copies, waits for them, and re-layouts: 3.27 us -> none
    pallas_call x1 -> x0, local copies, waits for them, and re-layouts: 3.25 us -> none  [mixer(): pl.pallas_call(functools.partial(mixer_kernel, rows, lon_cols), grid=(lat...]
    pallas_call x1, Pallas kernels: 19.8 us -> 17.2 us  [mixer(): pl.pallas_call(functools.partial(mixer_kernel, cols), grid=(lon_cols // c...]
where the time goes in v4:
time: 135 us; the launch traced here: 134 us
  Pallas kernels  134 us (99%)
    pallas_call x1, Pallas kernels, attention(): pl.pallas_call(functools.partial(attention_kernel, n, m, heads, lon_cols,...  117 us
    pallas_call x1, Pallas kernels, mixer(): pl.pallas_call(functools.partial(mixer_kernel, cols), grid=(lon_cols // c...  17.2 us

profile of v4, /device:TPU:25, one launch (start us, length us, event | category | flops | bytes accessed | tf_op | source)
XLA Modules:
  0.0 134.4 jit_solution(12439816193065312218)
XLA Ops:
  0.0 117.1 %shard_map.100 = (bf16[32,96,256]{2,1,0:T(8,128)(2,1)}, f32[2,2,256,128]{3,2,1,0:T(8,128)}) custom-call(bf16[28,96,256]{2,1,0:T(8,128)(2,1)} %bitcast.2, f32[3,256]{1,0:T(4,128)} %gains.3, bf16[256,768]{1,0:T(8,128)(2,1)} %wqkv1.1, bf16[256,256]{1,0:T(8,128)(2,1)} %wo1.1, bf16[256,768]{1,0:T(8,128)(2,1)} %wqkv2.1, bf16[256,256]{1,0:T(8,128)(2,1)} %wo2.1, ...), custom_call_target="tpu_custom_call" | custom-call | tf_op jit(solution)/shard_map/pallas_call | solution.py:338
  117.2 17.2 %shard_map.101 = bf16[28,96,256]{2,1,0:T(8,128)(2,1)} custom-call(bf16[32,96,256]{2,1,0:T(8,128)(2,1)} %get-tuple-element.7.wide, f32[2,2,256,128]{3,2,1,0:T(8,128)} %get-tuple-element.8.halo, f32[25,256]{1,0:T(8,128)} %taps.1, f32[3,256]{1,0:T(4,128)} %gains.3, bf16[256,2048]{1,0:T(8,128)(2,1)} %w_in.1, bf16[1024,256]{1,0:T(8,128)(2,1)} %w_down.1), custom_call_target="tpu_custom_call" | custom-call | tf_op jit(solution)/shard_map/pallas_call | solution.py:415

commit v5 on v4

--- a/solution.py
+++ b/solution.py
@@ -24,33 +24,43 @@
     return centred * lax.rsqrt(spread + EPSILON) * gains
 
 
-def attend(x, wqk, wvt, wout, factor_of, heads):
-    features = x.shape[-1]
+def attend(lines, wk, wqvt, wout, factors, heads):
+    length, features = lines[0].shape
     size = features // heads
-    qk = jnp.dot(x, wqk, preferred_element_type=F32).astype(BF16)
-    queries, keys = qk[:, :features], qk[:, features:]
-    values = lax.dot_general(wvt, x, NT, preferred_element_type=F32).astype(BF16)
+    together = max(1, min(heads, 5 * 2**20 // (4 * length * length)))
     lane = lax.broadcasted_iota(jnp.int32, (1, features), 1) // size
-    parts = []
-    for h in range(heads):
-        own = keys * (lane == h).astype(F32).astype(BF16)
-        scores = lax.dot_general(own, queries, NT, preferred_element_type=F32)
-        top = jnp.max(scores, 0, keepdims=True)
-        weights = jnp.exp2((scores - top) * (factor_of(h) * math.log2(math.e)))
-        total = jnp.sum(weights, 0, keepdims=True)
-        part = jnp.dot(
-            values[h * size : (h + 1) * size], weights.astype(BF16), preferred_element_type=F32
-        )
-        parts.append(part / total)
-    context = jnp.concatenate(parts, 0).astype(BF16)
-    return lax.dot_general(context, wout, TN, preferred_element_type=F32)
+    masks = [(lane == h).astype(F32).astype(BF16) for h in range(heads)]
+    all_keys = jnp.dot(jnp.concatenate(lines, 0), wk, preferred_element_type=F32).astype(BF16)
+    contexts = []
+    for number, x in enumerate(lines):
+        keys = all_keys[number * length : (number + 1) * length]
+        qvt = lax.dot_general(wqvt, x, NT, preferred_element_type=F32).astype(BF16)
+        queries, values = qvt[:features], qvt[features:]
+        parts = []
+        for base in range(0, heads, together):
+            group = range(base, min(heads, base + together))
+            own = jnp.concatenate([keys * masks[h] for h in group], 0)
+            scores = jnp.dot(own, queries, preferred_element_type=F32)
+            for h in group:
+                score = scores[(h - base) * length : (h - base + 1) * length]
+                top = jnp.max(score, 0, keepdims=True)
+                weights = jnp.exp2((score - top) * factors[h])
+                total = jnp.sum(weights, 0, keepdims=True)
+                part = jnp.dot(
+                    values[h * size : (h + 1) * size],
+                    weights.astype(BF16),
+                    preferred_element_type=F32,
+                )
+                parts.append(part * (1.0 / total))
+        contexts.append(jnp.concatenate(parts, 0).astype(BF16).T)
+    return jnp.dot(jnp.concatenate(contexts, 0), wout, preferred_element_type=F32)
 
 
 def attention_kernel(
     n, m, heads, lon_cols, chunk,
     x_ref, gains, wqkv1, wo1, wqkv2, wo2, scales,
     out_ref, halo_ref,
-    xs, recv, normed, stage, lines, mixed, obuf, ret, state, lsend, lrecv, lout, lret, wvt1, wvt2, erecv, rims, hsend, hrecv,
+    xs, recv, normed, stage, lines, mixed, obuf, ret, state, lsend, lrecv, lout, lret, wqvt1, wqvt2, erecv, rims, hsend, hrecv,
     fs, fr, bs, br, gs, gr, hs, hr, es, er, rs, rr,
 ):
     lat_rows, features = x_ref.shape[1:]
@@ -152,8 +162,14 @@
             forth(ch, d).start()
         recv[me, ch] = xs[me, ch]
 
-    wvt1[...] = wqkv1[:, split:].astype(F32).T.astype(BF16)
-    wvt2[...] = wqkv2[:, split:].astype(F32).T.astype(BF16)
+    for weight, turned in ((wqkv1, wqvt1), (wqkv2, wqvt2)):
+        turned[:features] = weight[:, :features].astype(F32).T.astype(BF16)
+        turned[features:] = weight[:, split:].astype(F32).T.astype(BF16)
+
+    log2e = math.log2(math.e)
+    factors1 = [scales[0, h] * log2e for h in range(heads)]
+    factors2 = [scales[1, h] * log2e for h in range(heads)]
+    at_once = chunk if n * lon_cols <= 256 else 1
 
     @pl.loop(0, chunks)
     def _(ch):
@@ -164,18 +180,22 @@
                 arrived = recv[j, ch, :, lanes(half)].astype(F32)
                 lines[half, j * tokens : (j + 1) * tokens, :] = arrived
 
-        @pl.loop(0, chunk)
-        def _(i):
-            place = pl.ds(i, n * lon_cols, stride=slot)
-            line = jnp.concatenate(
-                [lines.at[half][place, :] for half in range(halves)], 1
-            ).astype(BF16)
+        @pl.loop(0, chunk // at_once)
+        def _(step):
+            taken = []
+            for k in range(at_once):
+                place = pl.ds(step * at_once + k, n * lon_cols, stride=slot)
+                line = [lines.at[half][place, :] for half in range(halves)]
+                taken.append(jnp.concatenate(line, 1).astype(BF16))
             result = attend(
-                line, wqkv1[:, :split], wvt1[...], wo1[...], lambda h: scales[0, h], heads
+                taken, wqkv1[:, features:split], wqvt1[...], wo1[...], factors1, heads
             )
-            place = pl.ds(ch * chunk + i, n * lon_cols, stride=rows_own)
-            for half in range(halves):
-                mixed.at[half][place, :] = result[:, lanes(half)]
+            for k in range(at_once):
+                row = ch * chunk + step * at_once + k
+                place = pl.ds(row, n * lon_cols, stride=rows_own)
+                own = result[k * (n * lon_cols) : (k + 1) * (n * lon_cols)]
+                for half in range(halves):
+                    mixed.at[half][place, :] = own[:, lanes(half)]
 
     spare = segment - m * rows_own
 
@@ -221,7 +241,7 @@
             lat_forth(c, d).wait_recv()
         line = lrecv[:, c].reshape(m * lat_rows, features)
         result = attend(
-            line, wqkv2[:, :split], wvt2[...], wo2[...], lambda h: scales[1, h], heads
+            [line], wqkv2[:, features:split], wqvt2[...], wo2[...], factors2, heads
         )
         lout[:, c] = result.astype(BF16).reshape(m, lat_rows, features)
         for d in range(m - 1):
@@ -357,8 +377,8 @@
             pltpu.VMEM(groups, BF16),
             pltpu.VMEM(groups, BF16),
             pltpu.VMEM(groups, BF16),
-            pltpu.VMEM((features, features), BF16),
-            pltpu.VMEM((features, features), BF16),
+            pltpu.VMEM((2 * features, features), BF16),
+            pltpu.VMEM((2 * features, features), BF16),
             pltpu.VMEM((2, margin, lat_rows, features), BF16),
             pltpu.VMEM((2, halves, width * 8, LANES), F32),
             pltpu.VMEM((2, margin, width, features), BF16),

time: 135 us -> 116 us (0.86)
  Pallas kernels: 134 us -> 116 us
    pallas_call x1, Pallas kernels: 117 us -> 98.5 us  [attention(): pl.pallas_call(functools.partial(attention_kernel, n, m, heads, lon_cols,...]
where the time goes in v5:
time: 116 us
  Pallas kernels  116 us (100%)
    pallas_call x1, Pallas kernels, attention(): pl.pallas_call(functools.partial(attention_kernel, n, m, heads, lon_cols,...  98.5 us
    pallas_call x1, Pallas kernels, mixer(): pl.pallas_call(functools.partial(mixer_kernel, cols), grid=(lon_cols // c...  17.2 us

profile of v5, /device:TPU:25, one launch (start us, length us, event | category | flops | bytes accessed | tf_op | source)
XLA Modules:
  0.0 115.7 jit_solution(16618645115404948974)
XLA Ops:
  0.0 98.5 %shard_map.100 = (bf16[32,96,256]{2,1,0:T(8,128)(2,1)}, f32[2,2,256,128]{3,2,1,0:T(8,128)}) custom-call(bf16[28,96,256]{2,1,0:T(8,128)(2,1)} %bitcast.2, f32[3,256]{1,0:T(4,128)} %gains.3, bf16[256,768]{1,0:T(8,128)(2,1)} %wqkv1.1, bf16[256,256]{1,0:T(8,128)(2,1)} %wo1.1, bf16[256,768]{1,0:T(8,128)(2,1)} %wqkv2.1, bf16[256,256]{1,0:T(8,128)(2,1)} %wo2.1, ...), custom_call_target="tpu_custom_call" | custom-call | tf_op jit(solution)/shard_map/pallas_call | solution.py:358
  98.5 17.2 %shard_map.101 = bf16[28,96,256]{2,1,0:T(8,128)(2,1)} custom-call(bf16[32,96,256]{2,1,0:T(8,128)(2,1)} %get-tuple-element.7.wide, f32[2,2,256,128]{3,2,1,0:T(8,128)} %get-tuple-element.8.halo, f32[25,256]{1,0:T(8,128)} %taps.1, f32[3,256]{1,0:T(4,128)} %gains.3, bf16[256,2048]{1,0:T(8,128)(2,1)} %w_in.1, bf16[1024,256]{1,0:T(8,128)(2,1)} %w_down.1), custom_call_target="tpu_custom_call" | custom-call | tf_op jit(solution)/shard_map/pallas_call | solution.py:435

commit v6 on v5

--- a/solution.py
+++ b/solution.py
@@ -419,10 +419,17 @@
         term = term[:, 8 - margin + dy : 8 - margin + dy + rows]
         smoothed = term if smoothed is None else smoothed + term
     normed = layer_norm(smoothed.reshape(cols * rows, features), gains[2:3]).astype(BF16)
-    gate_up = jnp.dot(normed, w_in[...], preferred_element_type=F32)
-    half = gate_up[:, :hidden_len] * 0.5
-    hidden = (half * (1.0 + jnp.tanh(half)) * gate_up[:, hidden_len:]).astype(BF16)
-    update = jnp.dot(hidden, w_down[...], preferred_element_type=F32)
+    step = min(hidden_len, 256)
+    update = None
+    for base in range(0, hidden_len, step):
+        gate = jnp.dot(normed, w_in[:, base : base + step], preferred_element_type=F32)
+        up = jnp.dot(
+            normed, w_in[:, hidden_len + base : hidden_len + base + step], preferred_element_type=F32
+        )
+        half = gate * 0.5
+        hidden = (half * (1.0 + jnp.tanh(half)) * up).astype(BF16)
+        share = jnp.dot(hidden, w_down[base : base + step, :], preferred_element_type=F32)
+        update = share if update is None else update + share
     total = body[margin : margin + cols] + update.reshape(cols, rows, features)
     out[...] = total.astype(BF16)
 
@@ -430,7 +437,7 @@
 def mixer(widened, halo, conv_taps, norm_gains, mlp_in, mlp_down):
     width, lat_rows, features = widened.shape
     lon_cols = width - KERNEL + 1
-    cols = next(size for size in (4, 3, 2, 1) if lon_cols % size == 0)
+    cols = next(size for size in (7, 6, 5, 4, 3, 2, 1) if lon_cols % size == 0)
     vmem = pl.BlockSpec(memory_space=pltpu.VMEM)
     return pl.pallas_call(
         functools.partial(mixer_kernel, cols),

time: 116 us -> 114 us (0.983)
  Pallas kernels: 116 us -> 114 us
    pallas_call x1, Pallas kernels: 17.2 us -> 15.8 us  [mixer(): pl.pallas_call(functools.partial(mixer_kernel, cols), grid=(lon_cols // c...]
where the time goes in v6:
time: 114 us
  Pallas kernels  114 us (100%)
    pallas_call x1, Pallas kernels, attention(): pl.pallas_call(functools.partial(attention_kernel, n, m, heads, lon_cols,...  98.5 us
    pallas_call x1, Pallas kernels, mixer(): pl.pallas_call(functools.partial(mixer_kernel, cols), grid=(lon_cols // c...  15.8 us

profile of v6, /device:TPU:25, one launch (start us, length us, event | category | flops | bytes accessed | tf_op | source)
XLA Modules:
  0.0 114.3 jit_solution(7549216914303394475)
XLA Ops:
  0.0 98.5 %shard_map.100 = (bf16[32,96,256]{2,1,0:T(8,128)(2,1)}, f32[2,2,256,128]{3,2,1,0:T(8,128)}) custom-call(bf16[28,96,256]{2,1,0:T(8,128)(2,1)} %bitcast.2, f32[3,256]{1,0:T(4,128)} %gains.3, bf16[256,768]{1,0:T(8,128)(2,1)} %wqkv1.1, bf16[256,256]{1,0:T(8,128)(2,1)} %wo1.1, bf16[256,768]{1,0:T(8,128)(2,1)} %wqkv2.1, bf16[256,256]{1,0:T(8,128)(2,1)} %wo2.1, ...), custom_call_target="tpu_custom_call" | custom-call | tf_op jit(solution)/shard_map/pallas_call | solution.py:358
  98.5 15.8 %shard_map.101 = bf16[28,96,256]{2,1,0:T(8,128)(2,1)} custom-call(bf16[32,96,256]{2,1,0:T(8,128)(2,1)} %get-tuple-element.7.wide, f32[2,2,256,128]{3,2,1,0:T(8,128)} %get-tuple-element.8.halo, f32[25,256]{1,0:T(8,128)} %taps.1, f32[3,256]{1,0:T(4,128)} %gains.3, bf16[256,2048]{1,0:T(8,128)(2,1)} %w_in.1, bf16[1024,256]{1,0:T(8,128)(2,1)} %w_down.1), custom_call_target="tpu_custom_call" | custom-call | tf_op jit(solution)/shard_map/pallas_call | solution.py:442

commit v7 on v6

--- a/solution.py
+++ b/solution.py
@@ -139,10 +139,13 @@
     def lanes(half):
         return slice(half * LANES, (half + 1) * LANES)
 
-    @pl.loop(0, lon_cols)
-    def _(col):
-        block = layer_norm(x_ref[col].astype(F32), gains[0:1])
-        place = pl.ds(pl.multiple_of(col * lat_rows, 8), lat_rows)
+    several = next(size for size in (4, 3, 2, 1) if lon_cols % size == 0)
+
+    @pl.loop(0, lon_cols // several)
+    def _(i):
+        block = x_ref[pl.ds(i * several, several)].astype(F32)
+        block = layer_norm(block.reshape(several * lat_rows, features), gains[0:1])
+        place = pl.ds(pl.multiple_of(i * (several * lat_rows), 8), several * lat_rows)
         for half in range(halves):
             normed[half, place, :] = block[:, lanes(half)]
 

time: 114 us -> 111 us (0.974)
  Pallas kernels: 114 us -> 111 us
    pallas_call x1, Pallas kernels: 98.5 us -> 94.9 us  [attention(): pl.pallas_call(functools.partial(attention_kernel, n, m, heads, lon_cols,...]
where the time goes in v7:
time: 111 us
  Pallas kernels  111 us (100%)
    pallas_call x1, Pallas kernels, attention(): pl.pallas_call(functools.partial(attention_kernel, n, m, heads, lon_cols,...  94.9 us
    pallas_call x1, Pallas kernels, mixer(): pl.pallas_call(functools.partial(mixer_kernel, cols), grid=(lon_cols // c...  15.8 us

profile of v7, /device:TPU:25, one launch (start us, length us, event | category | flops | bytes accessed | tf_op | source)
XLA Modules:
  0.0 110.7 jit_solution(7113875654889528610)
XLA Ops:
  0.0 94.9 %shard_map.100 = (bf16[32,96,256]{2,1,0:T(8,128)(2,1)}, f32[2,2,256,128]{3,2,1,0:T(8,128)}) custom-call(bf16[28,96,256]{2,1,0:T(8,128)(2,1)} %bitcast.2, f32[3,256]{1,0:T(4,128)} %gains.3, bf16[256,768]{1,0:T(8,128)(2,1)} %wqkv1.1, bf16[256,256]{1,0:T(8,128)(2,1)} %wo1.1, bf16[256,768]{1,0:T(8,128)(2,1)} %wqkv2.1, bf16[256,256]{1,0:T(8,128)(2,1)} %wo2.1, ...), custom_call_target="tpu_custom_call" | custom-call | tf_op jit(solution)/shard_map/pallas_call | solution.py:361
  94.9 15.8 %shard_map.101 = bf16[28,96,256]{2,1,0:T(8,128)(2,1)} custom-call(bf16[32,96,256]{2,1,0:T(8,128)(2,1)} %get-tuple-element.7.wide, f32[2,2,256,128]{3,2,1,0:T(8,128)} %get-tuple-element.8.halo, f32[25,256]{1,0:T(8,128)} %taps.1, f32[3,256]{1,0:T(4,128)} %gains.3, bf16[256,2048]{1,0:T(8,128)(2,1)} %w_in.1, bf16[1024,256]{1,0:T(8,128)(2,1)} %w_down.1), custom_call_target="tpu_custom_call" | custom-call | tf_op jit(solution)/shard_map/pallas_call | solution.py:445

commit v8 on v7

--- a/solution.py
+++ b/solution.py
@@ -393,7 +393,7 @@
             dma((2,)), dma((2,)), dma((2,)), dma((2,)),
         ],
         compiler_params=pltpu.CompilerParams(
-            collective_id=0, has_side_effects=True, vmem_limit_bytes=60 * 2**20
+            collective_id=0, has_side_effects=True, vmem_limit_bytes=44 * 2**20
         ),
     )(fields, norm_gains, lon_qkv, lon_out, lat_qkv, lat_out, logit_scales)
 
@@ -448,7 +448,7 @@
         out_shape=jax.ShapeDtypeStruct((lon_cols, lat_rows, features), BF16),
         in_specs=[vmem] * 6,
         out_specs=pl.BlockSpec((cols, lat_rows, features), lambda i: (i, 0, 0)),
-        compiler_params=pltpu.CompilerParams(vmem_limit_bytes=60 * 2**20),
+        compiler_params=pltpu.CompilerParams(vmem_limit_bytes=40 * 2**20),
     )(widened, halo, conv_taps, norm_gains, mlp_in, mlp_down)
 
 

time: 111 us -> 113 us (1.018)
  local copies, waits for them, and re-layouts: 0 us -> 6.51 us
  Pallas kernels: 111 us -> 107 us
    unnamed x0 -> x20, local copies, waits for them, and re-layouts: none -> 6.51 us
    pallas_call x1, Pallas kernels: 94.9 us -> 92.5 us  [attention(): pl.pallas_call(functools.partial(attention_kernel, n, m, heads, lon_cols,...]
    pallas_call x1, Pallas kernels: 15.8 us -> 14 us  [mixer(): pl.pallas_call(functools.partial(mixer_kernel, cols), grid=(lon_cols // c...]
where the time goes in v8:
time: 113 us
  Pallas kernels  107 us (95%)
  local copies, waits for them, and re-layouts  6.51 us (6%)
    pallas_call x1, Pallas kernels, attention(): pl.pallas_call(functools.partial(attention_kernel, n, m, heads, lon_cols,...  92.5 us
    pallas_call x1, Pallas kernels, mixer(): pl.pallas_call(functools.partial(mixer_kernel, cols), grid=(lon_cols // c...  14 us
    unnamed x20, local copies, waits for them, and re-layouts  6.51 us

profile of v8, /device:TPU:25, one launch (start us, length us, event | category | flops | bytes accessed | tf_op | source)
XLA Modules:
  0.0 113.1 jit_solution(9783815913329529591)
XLA Ops:
  0.0 0.0 copy-start
  0.0 1.3 %copy-done = bf16[96,28,256]{2,0,1:T(8,128)(2,1)S(1)} copy-done((bf16[96,28,256]{2,0,1:T(8,128)(2,1)S(1)}, bf16[96,28,256]{2,0,1:T(8,128)(2,1)}, u32[]{:S(2)}) %copy-start) | copy-done | bytes 1376280
  1.3 0.0 copy-start.3
  1.3 1.0 copy-done.3
  2.3 0.0 copy-start.4
  2.3 1.0 copy-done.4
  3.3 0.0 copy-start.5
  3.3 0.9 copy-done.5
  4.2 0.0 copy-start.6
  4.2 0.9 copy-done.6
  5.1 0.0 copy-start.8
  5.1 0.7 copy-done.8
  5.8 0.0 copy-start.9
  5.8 0.7 copy-done.9
  6.5 0.0 copy-start.1
  6.5 0.0 copy-start.2
  6.5 0.0 copy-start.7
  6.5 92.5 %shard_map.100 = (bf16[32,96,256]{2,1,0:T(8,128)(2,1)S(1)}, f32[2,2,256,128]{3,2,1,0:T(8,128)S(1)}) custom-call(bf16[28,96,256]{2,1,0:T(8,128)(2,1)S(1)} %bitcast.2, f32[3,256]{1,0:T(4,128)S(1)} %copy-done.8, bf16[256,768]{1,0:T(8,128)(2,1)S(1)} %copy-done.3, bf16[256,256]{1,0:T(8,128)(2,1)S(1)} %copy-done.5, bf16[256,768]{1,0:T(8,128)(2,1)S(1)} %copy-done.4, ...), custom_call_target="tpu_custom_call" | custom-call | tf_op jit(solution)/shard_map/pallas_call | solution.py:361
  99.0 0.0 copy-done.1
  99.0 0.0 copy-done.2
  99.1 0.0 copy-done.7
  99.1 14.0 %shard_map.101 = bf16[28,96,256]{2,1,0:T(8,128)(2,1)} custom-call(bf16[32,96,256]{2,1,0:T(8,128)(2,1)S(1)} %get-tuple-element.7.wide, f32[2,2,256,128]{3,2,1,0:T(8,128)S(1)} %get-tuple-element.8.halo, f32[25,256]{1,0:T(8,128)S(1)} %copy-done.7, f32[3,256]{1,0:T(4,128)S(1)} %copy-done.8, bf16[256,2048]{1,0:T(8,128)(2,1)S(1)} %copy-done.1, ...), custom_call_target="tpu_custom_call" | custom-call | tf_op jit(solution)/shard_map/pallas_call | solution.py:445
Async XLA Ops:
  0.0 1.3 %copy-start = (bf16[96,28,256]{2,0,1:T(8,128)(2,1)S(1)}, bf16[96,28,256]{2,0,1:T(8,128)(2,1)}, u32[]{:S(2)}) copy-start(bf16[96,28,256]{2,0,1:T(8,128)(2,1)} %param.10) | copy-start | bytes 4128772
  1.3 1.0 copy-start.3
  2.3 1.0 copy-start.4
  3.3 0.9 copy-start.5
  4.2 0.9 copy-start.6
  5.1 0.7 copy-start.8
  5.8 0.7 copy-start.9
  6.5 92.5 %copy-start.1 = (bf16[256,2048]{1,0:T(8,128)(2,1)S(1)}, bf16[256,2048]{1,0:T(8,128)(2,1)}, u32[]{:S(2)}) copy-start(bf16[256,2048]{1,0:T(8,128)(2,1)} %w_in.1) | copy-start | bytes 3145732
  6.5 92.5 %copy-start.2 = (bf16[1024,256]{1,0:T(8,128)(2,1)S(1)}, bf16[1024,256]{1,0:T(8,128)(2,1)}, u32[]{:S(2)}) copy-start(bf16[1024,256]{1,0:T(8,128)(2,1)} %w_down.1) | copy-start | bytes 1572868
  6.5 92.5 %copy-start.7 = (f32[25,256]{1,0:T(8,128)S(1)}, f32[25,256]{1,0:T(8,128)}, u32[]{:S(2)}) copy-start(f32[25,256]{1,0:T(8,128)} %taps.1) | copy-start | bytes 76804
